TPU v7x, 128 devices: a whole 4x4x4 slice. The times are simulated.
128 devices in a mesh: lon: 32 (over z_lo, x, y), lat: 4 (over z_hi, core).
Axes of the slice: x: 4, y: 4, z: 4 (z_hi: 2, z_lo: 2; z = z_hi * 2 + z_lo), core: 2. Of those that a mesh axis runs over, the one named last changes fastest.
Arguments:
- initial_state: float32 [3, 3072, 4096], P(None, 'lat', 'lon'), may hold values from -6 to 6
- bottom_drag: float32 [3072, 4096], P('lat', 'lon'), may hold values from 0.05 to 1
- drag_direction: float32 [3072, 4096], P('lat', 'lon'), may hold values from -5 to 5
- land_mask: int32 [3072, 4096], P('lat', 'lon'), may hold values 0 or 1
- section_cells: int32 [8192], replicated, may hold values from 0 to 12582911
- section_sign: int32 [8192], replicated, may hold values from -1 to 1
Outputs:
- curvature: float32 [3072, 4096], P('lat', 'lon')
- final_state: float32 [3, 3072, 4096], P(None, 'lat', 'lon')
- final_tangent: float32 [3, 3072, 4096], P(None, 'lat', 'lon')
All inputs are finite; a program needn't handle non-finite values. No bound on the sum of `land_mask` on one device may be relied on, other than what follows from the above.
Results may differ from a plain program's by a relative error of at most 0.00002.
Values sent between devices are 32-bit elements; how exact they have to be, the bound alone decides.
A program may use at most 128 MiB of HBM per device.

v0:
```python
import jax
import jax.numpy as jnp
from jax import lax
from jax.sharding import PartitionSpec as P

ITERS = 6


wave_step = 0.4
coriolis = 0.25


def padded_2(shard, sides, width, wrap):
    for axis, dim in sides:
        size, length = (lax.axis_size(axis), shard.shape[dim])
        up = [(i, (i + 1) % size) for i in range(size if wrap else size - 1)]
        down = [(j, i) for i, j in up]
        last = lax.slice_in_dim(shard, length - width, length, axis=dim)
        first = lax.slice_in_dim(shard, 0, width, axis=dim)
        before = lax.ppermute(last, axis, up)
        after = lax.ppermute(first, axis, down)
        shard = jnp.concatenate([before, shard, after], axis=dim)
    return shard


def across(field):
    return 0.5 * (field[1:-1, 2:] - field[1:-1, :-2])


def along(field):
    return 0.5 * (field[2:, 1:-1] - field[:-2, 1:-1])


def advance(padded, drag_field, ocean):
    height = padded[0]
    zonal = padded[1]
    meridional = padded[2]
    height_mid = height[1:-1, 1:-1]
    zonal_mid = zonal[1:-1, 1:-1]
    merid_mid = meridional[1:-1, 1:-1]
    damping = ocean / (1.0 + drag_field)
    new_height = (height_mid - wave_step * (across(zonal) + along(meridional))) * ocean
    new_zonal = (zonal_mid - wave_step * across(height) + coriolis * merid_mid) * damping
    new_merid = (merid_mid - wave_step * along(height) - coriolis * zonal_mid) * damping
    return jnp.stack([new_height, new_zonal, new_merid])


def fold_row(top_row, signs):
    width = top_row.shape[1]
    whole = lax.all_gather(top_row, "lon", axis=1, tiled=True)
    flipped = whole[:, ::-1]
    offset = lax.axis_index("lon") * width
    mine = lax.dynamic_slice_in_dim(flipped, offset, width, 1)
    return mine * signs[:, None]


def pad_fields(packed, signs, top_band):
    count = packed.shape[0]
    columns = padded_2(packed, (("lon", 2),), 1, True)
    banded = padded_2(packed, (("lat", 1),), 1, False)
    folded = fold_row(packed[:, -1, :], signs)
    north_edge = jnp.where(top_band, folded, banded[:, -1, :])
    corner = jnp.zeros((count, 1, 1), packed.dtype)
    south = jnp.concatenate([corner, banded[:, :1, :], corner], axis=2)
    north = jnp.concatenate([corner, north_edge[:, None, :], corner], axis=2)
    return jnp.concatenate([south, columns, north], axis=1)


def pad_back(grads, signs, top_band):
    inner = grads[:, 1:-1, 1:-1]
    side_rims = jnp.stack([grads[:, 1:-1, 0], grads[:, 1:-1, -1]], axis=2)
    side_got = padded_2(side_rims, (("lon", 2),), 1, True)
    inner = inner.at[:, :, 0].add(side_got[:, :, 0])
    inner = inner.at[:, :, -1].add(side_got[:, :, 3])
    north_cot = grads[:, -1, 1:-1]
    edge_rims = jnp.stack([grads[:, 0, 1:-1], jnp.where(top_band, 0.0, north_cot)], axis=1)
    edge_got = padded_2(edge_rims, (("lat", 1),), 1, False)
    inner = inner.at[:, 0, :].add(edge_got[:, 0, :])
    inner = inner.at[:, -1, :].add(edge_got[:, 3, :])
    folded = fold_row(north_cot, signs)
    inner = inner.at[:, -1, :].add(jnp.where(top_band, folded, 0.0))
    return inner


def on_device(initial_state, bottom_drag, drag_direction, land_mask, section_cells, section_sign):
    ocean = land_mask.astype(jnp.float32)
    rows_dev, cols_dev = bottom_drag.shape
    total_cols = cols_dev * lax.axis_size("lon")
    top_band = lax.axis_index("lat") == lax.axis_size("lat") - 1
    signs = jnp.array([1.0, -1.0, -1.0, 1.0, -1.0, -1.0], jnp.float32)
    local_row = section_cells // total_cols - lax.axis_index("lat") * rows_dev
    local_col = section_cells % total_cols - lax.axis_index("lon") * cols_dev
    inside = (local_row >= 0) & (local_row < rows_dev) & (local_col >= 0) & (local_col < cols_dev)
    weights = (
        jnp.zeros((rows_dev, cols_dev), jnp.float32)
        .at[jnp.where(inside, local_row, 0), jnp.where(inside, local_col, 0)]
        .add(jnp.where(inside, section_sign.astype(jnp.float32), 0.0))
    )

    def stepper(padded_state, drag_field):
        return advance(padded_state, drag_field, ocean)

    def augmented(padded, drag_field):
        new_state, new_tangent = jax.jvp(
            stepper, (padded[:3], drag_field), (padded[3:], drag_direction)
        )
        return jnp.concatenate([new_state, new_tangent], axis=0)

    def forward_step(packed, unused):
        padded = pad_fields(packed, signs, top_band)
        return (augmented(padded, bottom_drag), padded)

    start = jnp.concatenate([initial_state * ocean[None], jnp.zeros_like(initial_state)], axis=0)
    finished, trail = lax.scan(forward_step, start, None, length=ITERS)

    def back_step(carry, padded):
        cotangent, total = carry
        unused_out, pullback = jax.vjp(augmented, padded, bottom_drag)
        grads, drag_grad = pullback(cotangent)
        return ((pad_back(grads, signs, top_band), total + drag_grad), None)

    seed = jnp.zeros_like(finished).at[5].set(weights)
    (unused_cot, curvature), unused_tail = lax.scan(
        back_step, (seed, jnp.zeros_like(bottom_drag)), trail, reverse=True
    )
    return (curvature, finished[:3], finished[3:])


def solution(mesh):
    return jax.shard_map(
        on_device,
        mesh=mesh,
        in_specs=(
            P(None, "lat", "lon"),
            P("lat", "lon"),
            P("lat", "lon"),
            P("lat", "lon"),
            P(),
            P(),
        ),
        out_specs=(P("lat", "lon"), P(None, "lat", "lon"), P(None, "lat", "lon")),
        check_vma=False,
    )
```

profile of v0, /device:TPU:1, one launch (start us, length us, event | category | flops | bytes accessed | tf_op | source)
XLA Modules:
  0.0 2175.3 jit_solution(18394670023096565494)
XLA Ops:
  4.0 56.8 %scatter_custom_fusion = f32[98304]{0:T(1024)S(1)} fusion(s32[8192]{0:T(1024)S(1)} %broadcast_select_fusion.1, f32[8192]{0:T(1024)S(1)} %get-tuple-element.665, f32[]{:T(128)} %constant.440.clone.1), kind=kCustom, calls=%fused_computation.162 | custom fusion | flops 8192 | bytes 393220
  67.5 732.1 %while.41 = (s32[]{:T(128)}, f32[6,768,128]{2,1,0:T(8,128)S(1)}, f32[6,6,770,130]{2,3,1,0:T(8,128)}, pred[]{:T(512)}, f32[768,128]{1,0:T(8,128)S(1)}, /*index=5*...) while((s32[]{:T(128)}, f32[6,768,128]{2,1,0:T(8,128)S(1)}, ...), condition=%wide.region_2.3_spmd.clone, body=%wide.region_1.2_spmd.sunk.clone.sunk | while | flops 7322264 | bytes 61938824 | solution.py:114
  68.9 3.2 collective-permute-start.1
  72.2 5.5 collective-permute-start
  81.4 5.4 collective-permute-start.2
  86.9 67.8 %all-gather.5 = f32[6,1,4096]{2,0,1:T(8,128)S(1)} all-gather(f32[6,1,128]{2,0,1:T(8,128)S(1)} %get-tuple-element.857), channel_id=2, replica_groups=mesh['lon'=32,'lat'=4] {'lon'}, dimensions={2}, use_global_device_ids=true | all-gather | bytes 101376 | tf_op jit(solution)/shard_map/while/body/eval_jaxpr/all_gather | solution.py:50
  154.7 10.6 rev.24
  171.9 3.9 bitcast_dynamic-update-slice_fusion.6
  187.0 14.3 collective-permute-start.1
  201.4 5.2 collective-permute-start
  211.8 66.3 %all-gather.5 = f32[6,1,4096]{2,0,1:T(8,128)S(1)} all-gather(f32[6,1,128]{2,0,1:T(8,128)S(1)} %get-tuple-element.857), channel_id=2, replica_groups=mesh['lon'=32,'lat'=4] {'lon'}, dimensions={2}, use_global_device_ids=true | all-gather | bytes 101376 | tf_op jit(solution)/shard_map/while/body/eval_jaxpr/all_gather | solution.py:50
  278.2 10.6 rev.24
  295.4 4.0 bitcast_dynamic-update-slice_fusion.6
  310.5 13.5 collective-permute-start.1
  324.0 5.2 collective-permute-start
  334.5 66.5 %all-gather.5 = f32[6,1,4096]{2,0,1:T(8,128)S(1)} all-gather(f32[6,1,128]{2,0,1:T(8,128)S(1)} %get-tuple-element.857), channel_id=2, replica_groups=mesh['lon'=32,'lat'=4] {'lon'}, dimensions={2}, use_global_device_ids=true | all-gather | bytes 101376 | tf_op jit(solution)/shard_map/while/body/eval_jaxpr/all_gather | solution.py:50
  401.0 10.6 rev.24
  418.2 4.0 bitcast_dynamic-update-slice_fusion.6
  433.4 13.2 collective-permute-start.1
  446.6 5.3 collective-permute-start
  457.1 66.5 %all-gather.5 = f32[6,1,4096]{2,0,1:T(8,128)S(1)} all-gather(f32[6,1,128]{2,0,1:T(8,128)S(1)} %get-tuple-element.857), channel_id=2, replica_groups=mesh['lon'=32,'lat'=4] {'lon'}, dimensions={2}, use_global_device_ids=true | all-gather | bytes 101376 | tf_op jit(solution)/shard_map/while/body/eval_jaxpr/all_gather | solution.py:50
  523.6 10.6 rev.24
  540.8 3.9 bitcast_dynamic-update-slice_fusion.6
  555.9 13.3 collective-permute-start.1
  569.2 5.3 collective-permute-start
  579.7 66.4 %all-gather.5 = f32[6,1,4096]{2,0,1:T(8,128)S(1)} all-gather(f32[6,1,128]{2,0,1:T(8,128)S(1)} %get-tuple-element.857), channel_id=2, replica_groups=mesh['lon'=32,'lat'=4] {'lon'}, dimensions={2}, use_global_device_ids=true | all-gather | bytes 101376 | tf_op jit(solution)/shard_map/while/body/eval_jaxpr/all_gather | solution.py:50
  646.1 10.6 rev.24
  663.4 3.9 bitcast_dynamic-update-slice_fusion.6
  678.5 13.3 collective-permute-start.1
  691.8 5.3 collective-permute-start
  702.3 66.4 %all-gather.5 = f32[6,1,4096]{2,0,1:T(8,128)S(1)} all-gather(f32[6,1,128]{2,0,1:T(8,128)S(1)} %get-tuple-element.857), channel_id=2, replica_groups=mesh['lon'=32,'lat'=4] {'lon'}, dimensions={2}, use_global_device_ids=true | all-gather | bytes 101376 | tf_op jit(solution)/shard_map/while/body/eval_jaxpr/all_gather | solution.py:50
  768.7 10.6 rev.24
  785.9 3.9 bitcast_dynamic-update-slice_fusion.6
  801.1 1369.2 %while.42 = (s32[]{:T(128)}, f32[6,768,128]{1,2,0:T(8,128)}, f32[768,128]{0,1:T(8,128)}, f32[768,128]{0,1:T(8,128)}, f32[768,128]{0,1:T(8,128)S(1)}, /*index=5*/...) while((s32[]{:T(128)}, f32[6,768,128]{1,2,0:T(8,128)}, ...), condition=%wide.region_4.5_spmd.clone.clone, body=%wide.region_3.4_spmd.sunk.clone.clone.sunk | while | flops 12170880 | bytes 65810144 | solution.py:123
  809.2 16.7 collective-permute-start.6
  828.0 175.8 %all-gather.6 = f32[6,1,4096]{1,2,0:T(8,128)} all-gather(f32[6,1,128]{1,2,0:T(8,128)S(1)} %get-tuple-element.914), channel_id=3, replica_groups=mesh['lon'=32,'lat'=4] {'lon'}, dimensions={2}, use_global_device_ids=true | all-gather | bytes 101376 | tf_op jit(solution)/shard_map/while/body/eval_jaxpr/all_gather | solution.py:50
  1003.8 7.9 reduce.26
  1016.1 2.7 fusion.115
  1030.8 2.4 scatter-add.56
  1043.5 15.0 collective-permute-start.6
  1061.9 178.3 %all-gather.6 = f32[6,1,4096]{1,2,0:T(8,128)} all-gather(f32[6,1,128]{1,2,0:T(8,128)S(1)} %get-tuple-element.914), channel_id=3, replica_groups=mesh['lon'=32,'lat'=4] {'lon'}, dimensions={2}, use_global_device_ids=true | all-gather | bytes 101376 | tf_op jit(solution)/shard_map/while/body/eval_jaxpr/all_gather | solution.py:50
  1240.2 7.9 reduce.26
  1252.5 2.7 fusion.115
  1267.2 2.4 scatter-add.56
  1279.9 5.5 collective-permute-start.6
  1288.9 171.8 %all-gather.6 = f32[6,1,4096]{1,2,0:T(8,128)} all-gather(f32[6,1,128]{1,2,0:T(8,128)S(1)} %get-tuple-element.914), channel_id=3, replica_groups=mesh['lon'=32,'lat'=4] {'lon'}, dimensions={2}, use_global_device_ids=true | all-gather | bytes 101376 | tf_op jit(solution)/shard_map/while/body/eval_jaxpr/all_gather | solution.py:50
  1460.6 7.9 reduce.26
  1472.9 2.7 fusion.115
  1488.6 2.4 scatter-add.56
  1501.3 11.1 collective-permute-start.6
  1515.8 172.2 %all-gather.6 = f32[6,1,4096]{1,2,0:T(8,128)} all-gather(f32[6,1,128]{1,2,0:T(8,128)S(1)} %get-tuple-element.914), channel_id=3, replica_groups=mesh['lon'=32,'lat'=4] {'lon'}, dimensions={2}, use_global_device_ids=true | all-gather | bytes 101376 | tf_op jit(solution)/shard_map/while/body/eval_jaxpr/all_gather | solution.py:50
  1688.1 7.9 reduce.26
  1700.3 2.7 fusion.115
  1715.0 2.4 scatter-add.56
  1727.8 11.4 collective-permute-start.6
  1742.6 170.8 %all-gather.6 = f32[6,1,4096]{1,2,0:T(8,128)} all-gather(f32[6,1,128]{1,2,0:T(8,128)S(1)} %get-tuple-element.914), channel_id=3, replica_groups=mesh['lon'=32,'lat'=4] {'lon'}, dimensions={2}, use_global_device_ids=true | all-gather | bytes 101376 | tf_op jit(solution)/shard_map/while/body/eval_jaxpr/all_gather | solution.py:50
  1913.4 7.9 reduce.26
  1925.7 2.7 fusion.115
  1940.4 2.4 scatter-add.56
  1953.1 12.3 collective-permute-start.6
  1968.8 169.6 %all-gather.6 = f32[6,1,4096]{1,2,0:T(8,128)} all-gather(f32[6,1,128]{1,2,0:T(8,128)S(1)} %get-tuple-element.914), channel_id=3, replica_groups=mesh['lon'=32,'lat'=4] {'lon'}, dimensions={2}, use_global_device_ids=true | all-gather | bytes 101376 | tf_op jit(solution)/shard_map/while/body/eval_jaxpr/all_gather | solution.py:50
  2138.5 7.9 reduce.26
  2150.7 2.7 fusion.115
  2172.2 3.2 fusion.89
  (511 shorter events, 330.9 us)
Async XLA Ops:
  0.6 61.9 %copy-start.13 = (s32[768,128]{1,0:T(8,128)S(1)}, s32[768,128]{1,0:T(8,128)}, u32[]{:S(2)}) copy-start(s32[768,128]{1,0:T(8,128)} %param.26) | copy-start | bytes 1179652
  67.5 97.8 %copy-start.8 = (f32[768,128]{1,0:T(8,128)}, f32[768,128]{1,0:T(8,128)S(1)}, u32[]{:S(2)}) copy-start(f32[768,128]{1,0:T(8,128)S(1)} %get-tuple-element.958) | copy-start | bytes 1179652 | tf_op jit(solution)/shard_map/while
  68.9 98.9 %collective-permute-start.1 = (f32[6,1,128]{2,0,1:T(8,128)S(1)}, f32[6,1,128]{2,0,1:T(8,128)S(1)}, u32[]{:S(2)}, u32[]{:S(2)}) collective-permute-start(f32[6,1,128]{2,0,1:T(8,128)S(1)} %get-tuple-element.858), channel_id=1, source_target_pairs={{1,0},{2,1},{3,2},{5,4},{6,5},{7,6},{9,8},{10,9},{11,10},{13,12},{... | collective-permute-start | bytes 9224 | tf_op jit(solution)/shard_map/while/body/eval_jaxpr/ppermute | solution.py:21
  72.2 96.5 %collective-permute-start = (f32[6,1,128]{2,0,1:T(8,128)S(1)}, f32[6,1,128]{2,0,1:T(8,128)S(1)}, u32[]{:S(2)}, u32[]{:S(2)}) collective-permute-start(f32[6,1,128]{2,0,1:T(8,128)S(1)} %get-tuple-element.857), channel_id=1, source_target_pairs={{0,1},{1,2},{2,3},{4,5},{5,6},{6,7},{8,9},{9,10},{10,11},{12,13},{... | collective-permute-start | bytes 9224 | tf_op jit(solution)/shard_map/while/body/eval_jaxpr/ppermute | solution.py:20
  79.7 92.3 %copy-start.1 = (f32[6,768,128]{1,2,0:T(8,128)S(1)}, f32[6,768,128]{1,2,0:T(8,128)}, u32[]{:S(2)}) copy-start(f32[6,768,128]{1,2,0:T(8,128)} %copy.176) | copy-start | bytes 7077892 | tf_op jit(solution)/shard_map/while
  81.4 90.5 %collective-permute-start.2 = (f32[6,768,1]{1,2,0:T(1,128)}, f32[6,768,1]{1,2,0:T(1,128)}, u32[]{:S(2)}, u32[]{:S(2)}) collective-permute-start(f32[6,768,1]{1,2,0:T(1,128)} %get-tuple-element.860), channel_id=1, source_target_pairs={{4,0},{8,4},{12,8},{16,12},{20,16},{24,20},{28,24},{32,28},{36,32}... | collective-permute-start | bytes 55304 | tf_op jit(solution)/shard_map/while/body/eval_jaxpr/ppermute | solution.py:21
  86.9 85.1 %collective-permute-start.3 = (f32[6,768,1]{1,2,0:T(1,128)}, f32[6,768,1]{1,2,0:T(1,128)}, u32[]{:S(2)}, u32[]{:S(2)}) collective-permute-start(f32[6,768,1]{1,2,0:T(1,128)} %get-tuple-element.861), channel_id=1, source_target_pairs={{0,4},{4,8},{8,12},{12,16},{16,20},{20,24},{24,28},{28,32},{32,36}... | collective-permute-start | bytes 55304 | tf_op jit(solution)/shard_map/while/body/eval_jaxpr/ppermute | solution.py:20
  185.6 103.2 %copy-start.8 = (f32[768,128]{1,0:T(8,128)}, f32[768,128]{1,0:T(8,128)S(1)}, u32[]{:S(2)}) copy-start(f32[768,128]{1,0:T(8,128)S(1)} %get-tuple-element.958) | copy-start | bytes 1179652 | tf_op jit(solution)/shard_map/while
  187.0 104.3 %collective-permute-start.1 = (f32[6,1,128]{2,0,1:T(8,128)S(1)}, f32[6,1,128]{2,0,1:T(8,128)S(1)}, u32[]{:S(2)}, u32[]{:S(2)}) collective-permute-start(f32[6,1,128]{2,0,1:T(8,128)S(1)} %get-tuple-element.858), channel_id=1, source_target_pairs={{1,0},{2,1},{3,2},{5,4},{6,5},{7,6},{9,8},{10,9},{11,10},{13,12},{... | collective-permute-start | bytes 9224 | tf_op jit(solution)/shard_map/while/body/eval_jaxpr/ppermute | solution.py:21
  201.4 90.7 %collective-permute-start = (f32[6,1,128]{2,0,1:T(8,128)S(1)}, f32[6,1,128]{2,0,1:T(8,128)S(1)}, u32[]{:S(2)}, u32[]{:S(2)}) collective-permute-start(f32[6,1,128]{2,0,1:T(8,128)S(1)} %get-tuple-element.857), channel_id=1, source_target_pairs={{0,1},{1,2},{2,3},{4,5},{5,6},{6,7},{8,9},{9,10},{10,11},{12,13},{... | collective-permute-start | bytes 9224 | tf_op jit(solution)/shard_map/while/body/eval_jaxpr/ppermute | solution.py:20
  208.6 86.8 %copy-start.1 = (f32[6,768,128]{1,2,0:T(8,128)S(1)}, f32[6,768,128]{1,2,0:T(8,128)}, u32[]{:S(2)}) copy-start(f32[6,768,128]{1,2,0:T(8,128)} %copy.176) | copy-start | bytes 7077892 | tf_op jit(solution)/shard_map/while
  210.3 85.0 %collective-permute-start.2 = (f32[6,768,1]{1,2,0:T(1,128)}, f32[6,768,1]{1,2,0:T(1,128)}, u32[]{:S(2)}, u32[]{:S(2)}) collective-permute-start(f32[6,768,1]{1,2,0:T(1,128)} %get-tuple-element.860), channel_id=1, source_target_pairs={{4,0},{8,4},{12,8},{16,12},{20,16},{24,20},{28,24},{32,28},{36,32}... | collective-permute-start | bytes 55304 | tf_op jit(solution)/shard_map/while/body/eval_jaxpr/ppermute | solution.py:21
  210.3 85.0 %collective-permute-start.3 = (f32[6,768,1]{1,2,0:T(1,128)}, f32[6,768,1]{1,2,0:T(1,128)}, u32[]{:S(2)}, u32[]{:S(2)}) collective-permute-start(f32[6,768,1]{1,2,0:T(1,128)} %get-tuple-element.861), channel_id=1, source_target_pairs={{0,4},{4,8},{8,12},{12,16},{16,20},{20,24},{24,28},{28,32},{32,36}... | collective-permute-start | bytes 55304 | tf_op jit(solution)/shard_map/while/body/eval_jaxpr/ppermute | solution.py:20
  309.1 102.5 %copy-start.8 = (f32[768,128]{1,0:T(8,128)}, f32[768,128]{1,0:T(8,128)S(1)}, u32[]{:S(2)}) copy-start(f32[768,128]{1,0:T(8,128)S(1)} %get-tuple-element.958) | copy-start | bytes 1179652 | tf_op jit(solution)/shard_map/while
  310.5 103.6 %collective-permute-start.1 = (f32[6,1,128]{2,0,1:T(8,128)S(1)}, f32[6,1,128]{2,0,1:T(8,128)S(1)}, u32[]{:S(2)}, u32[]{:S(2)}) collective-permute-start(f32[6,1,128]{2,0,1:T(8,128)S(1)} %get-tuple-element.858), channel_id=1, source_target_pairs={{1,0},{2,1},{3,2},{5,4},{6,5},{7,6},{9,8},{10,9},{11,10},{13,12},{... | collective-permute-start | bytes 9224 | tf_op jit(solution)/shard_map/while/body/eval_jaxpr/ppermute | solution.py:21
  324.0 90.9 %collective-permute-start = (f32[6,1,128]{2,0,1:T(8,128)S(1)}, f32[6,1,128]{2,0,1:T(8,128)S(1)}, u32[]{:S(2)}, u32[]{:S(2)}) collective-permute-start(f32[6,1,128]{2,0,1:T(8,128)S(1)} %get-tuple-element.857), channel_id=1, source_target_pairs={{0,1},{1,2},{2,3},{4,5},{5,6},{6,7},{8,9},{9,10},{10,11},{12,13},{... | collective-permute-start | bytes 9224 | tf_op jit(solution)/shard_map/while/body/eval_jaxpr/ppermute | solution.py:20
  331.2 87.0 %copy-start.1 = (f32[6,768,128]{1,2,0:T(8,128)S(1)}, f32[6,768,128]{1,2,0:T(8,128)}, u32[]{:S(2)}) copy-start(f32[6,768,128]{1,2,0:T(8,128)} %copy.176) | copy-start | bytes 7077892 | tf_op jit(solution)/shard_map/while
  333.0 85.2 %collective-permute-start.2 = (f32[6,768,1]{1,2,0:T(1,128)}, f32[6,768,1]{1,2,0:T(1,128)}, u32[]{:S(2)}, u32[]{:S(2)}) collective-permute-start(f32[6,768,1]{1,2,0:T(1,128)} %get-tuple-element.860), channel_id=1, source_target_pairs={{4,0},{8,4},{12,8},{16,12},{20,16},{24,20},{28,24},{32,28},{36,32}... | collective-permute-start | bytes 55304 | tf_op jit(solution)/shard_map/while/body/eval_jaxpr/ppermute | solution.py:21
  333.0 85.2 %collective-permute-start.3 = (f32[6,768,1]{1,2,0:T(1,128)}, f32[6,768,1]{1,2,0:T(1,128)}, u32[]{:S(2)}, u32[]{:S(2)}) collective-permute-start(f32[6,768,1]{1,2,0:T(1,128)} %get-tuple-element.861), channel_id=1, source_target_pairs={{0,4},{4,8},{8,12},{12,16},{16,20},{20,24},{24,28},{28,32},{32,36}... | collective-permute-start | bytes 55304 | tf_op jit(solution)/shard_map/while/body/eval_jaxpr/ppermute | solution.py:20
  431.9 102.3 %copy-start.8 = (f32[768,128]{1,0:T(8,128)}, f32[768,128]{1,0:T(8,128)S(1)}, u32[]{:S(2)}) copy-start(f32[768,128]{1,0:T(8,128)S(1)} %get-tuple-element.958) | copy-start | bytes 1179652 | tf_op jit(solution)/shard_map/while
  433.4 103.4 %collective-permute-start.1 = (f32[6,1,128]{2,0,1:T(8,128)S(1)}, f32[6,1,128]{2,0,1:T(8,128)S(1)}, u32[]{:S(2)}, u32[]{:S(2)}) collective-permute-start(f32[6,1,128]{2,0,1:T(8,128)S(1)} %get-tuple-element.858), channel_id=1, source_target_pairs={{1,0},{2,1},{3,2},{5,4},{6,5},{7,6},{9,8},{10,9},{11,10},{13,12},{... | collective-permute-start | bytes 9224 | tf_op jit(solution)/shard_map/while/body/eval_jaxpr/ppermute | solution.py:21
  446.6 90.9 %collective-permute-start = (f32[6,1,128]{2,0,1:T(8,128)S(1)}, f32[6,1,128]{2,0,1:T(8,128)S(1)}, u32[]{:S(2)}, u32[]{:S(2)}) collective-permute-start(f32[6,1,128]{2,0,1:T(8,128)S(1)} %get-tuple-element.857), channel_id=1, source_target_pairs={{0,1},{1,2},{2,3},{4,5},{5,6},{6,7},{8,9},{9,10},{10,11},{12,13},{... | collective-permute-start | bytes 9224 | tf_op jit(solution)/shard_map/while/body/eval_jaxpr/ppermute | solution.py:20
  453.8 87.0 %copy-start.1 = (f32[6,768,128]{1,2,0:T(8,128)S(1)}, f32[6,768,128]{1,2,0:T(8,128)}, u32[]{:S(2)}) copy-start(f32[6,768,128]{1,2,0:T(8,128)} %copy.176) | copy-start | bytes 7077892 | tf_op jit(solution)/shard_map/while
  455.6 85.2 %collective-permute-start.2 = (f32[6,768,1]{1,2,0:T(1,128)}, f32[6,768,1]{1,2,0:T(1,128)}, u32[]{:S(2)}, u32[]{:S(2)}) collective-permute-start(f32[6,768,1]{1,2,0:T(1,128)} %get-tuple-element.860), channel_id=1, source_target_pairs={{4,0},{8,4},{12,8},{16,12},{20,16},{24,20},{28,24},{32,28},{36,32}... | collective-permute-start | bytes 55304 | tf_op jit(solution)/shard_map/while/body/eval_jaxpr/ppermute | solution.py:21
  455.6 85.2 %collective-permute-start.3 = (f32[6,768,1]{1,2,0:T(1,128)}, f32[6,768,1]{1,2,0:T(1,128)}, u32[]{:S(2)}, u32[]{:S(2)}) collective-permute-start(f32[6,768,1]{1,2,0:T(1,128)} %get-tuple-element.861), channel_id=1, source_target_pairs={{0,4},{4,8},{8,12},{12,16},{16,20},{20,24},{24,28},{28,32},{32,36}... | collective-permute-start | bytes 55304 | tf_op jit(solution)/shard_map/while/body/eval_jaxpr/ppermute | solution.py:20
  554.5 102.3 %copy-start.8 = (f32[768,128]{1,0:T(8,128)}, f32[768,128]{1,0:T(8,128)S(1)}, u32[]{:S(2)}) copy-start(f32[768,128]{1,0:T(8,128)S(1)} %get-tuple-element.958) | copy-start | bytes 1179652 | tf_op jit(solution)/shard_map/while
  555.9 103.4 %collective-permute-start.1 = (f32[6,1,128]{2,0,1:T(8,128)S(1)}, f32[6,1,128]{2,0,1:T(8,128)S(1)}, u32[]{:S(2)}, u32[]{:S(2)}) collective-permute-start(f32[6,1,128]{2,0,1:T(8,128)S(1)} %get-tuple-element.858), channel_id=1, source_target_pairs={{1,0},{2,1},{3,2},{5,4},{6,5},{7,6},{9,8},{10,9},{11,10},{13,12},{... | collective-permute-start | bytes 9224 | tf_op jit(solution)/shard_map/while/body/eval_jaxpr/ppermute | solution.py:21
  569.2 90.9 %collective-permute-start = (f32[6,1,128]{2,0,1:T(8,128)S(1)}, f32[6,1,128]{2,0,1:T(8,128)S(1)}, u32[]{:S(2)}, u32[]{:S(2)}) collective-permute-start(f32[6,1,128]{2,0,1:T(8,128)S(1)} %get-tuple-element.857), channel_id=1, source_target_pairs={{0,1},{1,2},{2,3},{4,5},{5,6},{6,7},{8,9},{9,10},{10,11},{12,13},{... | collective-permute-start | bytes 9224 | tf_op jit(solution)/shard_map/while/body/eval_jaxpr/ppermute | solution.py:20
  576.4 86.9 %copy-start.1 = (f32[6,768,128]{1,2,0:T(8,128)S(1)}, f32[6,768,128]{1,2,0:T(8,128)}, u32[]{:S(2)}) copy-start(f32[6,768,128]{1,2,0:T(8,128)} %copy.176) | copy-start | bytes 7077892 | tf_op jit(solution)/shard_map/while
  578.2 85.1 %collective-permute-start.2 = (f32[6,768,1]{1,2,0:T(1,128)}, f32[6,768,1]{1,2,0:T(1,128)}, u32[]{:S(2)}, u32[]{:S(2)}) collective-permute-start(f32[6,768,1]{1,2,0:T(1,128)} %get-tuple-element.860), channel_id=1, source_target_pairs={{4,0},{8,4},{12,8},{16,12},{20,16},{24,20},{28,24},{32,28},{36,32}... | collective-permute-start | bytes 55304 | tf_op jit(solution)/shard_map/while/body/eval_jaxpr/ppermute | solution.py:21
  578.2 85.1 %collective-permute-start.3 = (f32[6,768,1]{1,2,0:T(1,128)}, f32[6,768,1]{1,2,0:T(1,128)}, u32[]{:S(2)}, u32[]{:S(2)}) collective-permute-start(f32[6,768,1]{1,2,0:T(1,128)} %get-tuple-element.861), channel_id=1, source_target_pairs={{0,4},{4,8},{8,12},{12,16},{16,20},{20,24},{24,28},{28,32},{32,36}... | collective-permute-start | bytes 55304 | tf_op jit(solution)/shard_map/while/body/eval_jaxpr/ppermute | solution.py:20
  677.0 102.3 %copy-start.8 = (f32[768,128]{1,0:T(8,128)}, f32[768,128]{1,0:T(8,128)S(1)}, u32[]{:S(2)}) copy-start(f32[768,128]{1,0:T(8,128)S(1)} %get-tuple-element.958) | copy-start | bytes 1179652 | tf_op jit(solution)/shard_map/while
  678.5 103.4 %collective-permute-start.1 = (f32[6,1,128]{2,0,1:T(8,128)S(1)}, f32[6,1,128]{2,0,1:T(8,128)S(1)}, u32[]{:S(2)}, u32[]{:S(2)}) collective-permute-start(f32[6,1,128]{2,0,1:T(8,128)S(1)} %get-tuple-element.858), channel_id=1, source_target_pairs={{1,0},{2,1},{3,2},{5,4},{6,5},{7,6},{9,8},{10,9},{11,10},{13,12},{... | collective-permute-start | bytes 9224 | tf_op jit(solution)/shard_map/while/body/eval_jaxpr/ppermute | solution.py:21
  691.8 90.9 %collective-permute-start = (f32[6,1,128]{2,0,1:T(8,128)S(1)}, f32[6,1,128]{2,0,1:T(8,128)S(1)}, u32[]{:S(2)}, u32[]{:S(2)}) collective-permute-start(f32[6,1,128]{2,0,1:T(8,128)S(1)} %get-tuple-element.857), channel_id=1, source_target_pairs={{0,1},{1,2},{2,3},{4,5},{5,6},{6,7},{8,9},{9,10},{10,11},{12,13},{... | collective-permute-start | bytes 9224 | tf_op jit(solution)/shard_map/while/body/eval_jaxpr/ppermute | solution.py:20
  699.0 86.9 %copy-start.1 = (f32[6,768,128]{1,2,0:T(8,128)S(1)}, f32[6,768,128]{1,2,0:T(8,128)}, u32[]{:S(2)}) copy-start(f32[6,768,128]{1,2,0:T(8,128)} %copy.176) | copy-start | bytes 7077892 | tf_op jit(solution)/shard_map/while
  700.8 85.1 %collective-permute-start.2 = (f32[6,768,1]{1,2,0:T(1,128)}, f32[6,768,1]{1,2,0:T(1,128)}, u32[]{:S(2)}, u32[]{:S(2)}) collective-permute-start(f32[6,768,1]{1,2,0:T(1,128)} %get-tuple-element.860), channel_id=1, source_target_pairs={{4,0},{8,4},{12,8},{16,12},{20,16},{24,20},{28,24},{32,28},{36,32}... | collective-permute-start | bytes 55304 | tf_op jit(solution)/shard_map/while/body/eval_jaxpr/ppermute | solution.py:21
  700.8 85.1 %collective-permute-start.3 = (f32[6,768,1]{1,2,0:T(1,128)}, f32[6,768,1]{1,2,0:T(1,128)}, u32[]{:S(2)}, u32[]{:S(2)}) collective-permute-start(f32[6,768,1]{1,2,0:T(1,128)} %get-tuple-element.861), channel_id=1, source_target_pairs={{0,4},{4,8},{8,12},{12,16},{16,20},{20,24},{24,28},{28,32},{32,36}... | collective-permute-start | bytes 55304 | tf_op jit(solution)/shard_map/while/body/eval_jaxpr/ppermute | solution.py:20
  809.2 217.0 %collective-permute-start.6 = (f32[6,1,128]{1,2,0:T(8,128)}, f32[6,1,128]{1,2,0:T(8,128)}, u32[]{:S(2)}, u32[]{:S(2)}) collective-permute-start(f32[6,1,128]{1,2,0:T(8,128)} %get-tuple-element.913), channel_id=1, source_target_pairs={{0,1},{1,2},{2,3},{4,5},{5,6},{6,7},{8,9},{9,10},{10,11},{12,13},{... | collective-permute-start | bytes 9224 | tf_op jit(solution)/shard_map/while/body/eval_jaxpr/ppermute | solution.py:20
  826.0 192.9 %collective-permute-start.4 = (f32[6,768,1]{1,2,0:T(1,128)S(1)}, f32[6,768,1]{1,2,0:T(1,128)S(1)}, u32[]{:S(2)}, u32[]{:S(2)}) collective-permute-start(f32[6,768,1]{1,2,0:T(1,128)S(1)} %fusion.112), channel_id=1, source_target_pairs={{0,4},{4,8},{8,12},{12,16},{16,20},{20,24},{24,28},{28,32},{32,36}... | collective-permute-start | bytes 55304 | tf_op jit(solution)/shard_map/while/body/eval_jaxpr/ppermute | solution.py:20
  826.1 203.5 %collective-permute-start.7 = (f32[6,1,128]{1,2,0:T(8,128)}, f32[6,1,128]{1,2,0:T(8,128)}, u32[]{:S(2)}, u32[]{:S(2)}) collective-permute-start(f32[6,1,128]{1,2,0:T(8,128)} %get-tuple-element.915), channel_id=1, source_target_pairs={{1,0},{2,1},{3,2},{5,4},{6,5},{7,6},{9,8},{10,9},{11,10},{13,12},{... | collective-permute-start | bytes 9224 | tf_op jit(solution)/shard_map/while/body/eval_jaxpr/ppermute | solution.py:21
  1019.0 4.6 collective-permute-start.5
  1027.4 8.2 copy-start.7
  1043.5 219.1 %collective-permute-start.6 = (f32[6,1,128]{1,2,0:T(8,128)}, f32[6,1,128]{1,2,0:T(8,128)}, u32[]{:S(2)}, u32[]{:S(2)}) collective-permute-start(f32[6,1,128]{1,2,0:T(8,128)} %get-tuple-element.913), channel_id=1, source_target_pairs={{0,1},{1,2},{2,3},{4,5},{5,6},{6,7},{8,9},{9,10},{10,11},{12,13},{... | collective-permute-start | bytes 9224 | tf_op jit(solution)/shard_map/while/body/eval_jaxpr/ppermute | solution.py:20
  1058.6 196.7 %collective-permute-start.4 = (f32[6,768,1]{1,2,0:T(1,128)S(1)}, f32[6,768,1]{1,2,0:T(1,128)S(1)}, u32[]{:S(2)}, u32[]{:S(2)}) collective-permute-start(f32[6,768,1]{1,2,0:T(1,128)S(1)} %fusion.112), channel_id=1, source_target_pairs={{0,4},{4,8},{8,12},{12,16},{16,20},{20,24},{24,28},{28,32},{32,36}... | collective-permute-start | bytes 55304 | tf_op jit(solution)/shard_map/while/body/eval_jaxpr/ppermute | solution.py:20
  1060.0 205.9 %collective-permute-start.7 = (f32[6,1,128]{1,2,0:T(8,128)}, f32[6,1,128]{1,2,0:T(8,128)}, u32[]{:S(2)}, u32[]{:S(2)}) collective-permute-start(f32[6,1,128]{1,2,0:T(8,128)} %get-tuple-element.915), channel_id=1, source_target_pairs={{1,0},{2,1},{3,2},{5,4},{6,5},{7,6},{9,8},{10,9},{11,10},{13,12},{... | collective-permute-start | bytes 9224 | tf_op jit(solution)/shard_map/while/body/eval_jaxpr/ppermute | solution.py:21
  1255.4 4.6 collective-permute-start.5
  1263.8 8.2 copy-start.7
  1279.9 204.1 %collective-permute-start.6 = (f32[6,1,128]{1,2,0:T(8,128)}, f32[6,1,128]{1,2,0:T(8,128)}, u32[]{:S(2)}, u32[]{:S(2)}) collective-permute-start(f32[6,1,128]{1,2,0:T(8,128)} %get-tuple-element.913), channel_id=1, source_target_pairs={{0,1},{1,2},{2,3},{4,5},{5,6},{6,7},{8,9},{9,10},{10,11},{12,13},{... | collective-permute-start | bytes 9224 | tf_op jit(solution)/shard_map/while/body/eval_jaxpr/ppermute | solution.py:20
  1285.6 190.1 %collective-permute-start.4 = (f32[6,768,1]{1,2,0:T(1,128)S(1)}, f32[6,768,1]{1,2,0:T(1,128)S(1)}, u32[]{:S(2)}, u32[]{:S(2)}) collective-permute-start(f32[6,768,1]{1,2,0:T(1,128)S(1)} %fusion.112), channel_id=1, source_target_pairs={{0,4},{4,8},{8,12},{12,16},{16,20},{20,24},{24,28},{28,32},{32,36}... | collective-permute-start | bytes 55304 | tf_op jit(solution)/shard_map/while/body/eval_jaxpr/ppermute | solution.py:20
  1287.0 200.3 %collective-permute-start.7 = (f32[6,1,128]{1,2,0:T(8,128)}, f32[6,1,128]{1,2,0:T(8,128)}, u32[]{:S(2)}, u32[]{:S(2)}) collective-permute-start(f32[6,1,128]{1,2,0:T(8,128)} %get-tuple-element.915), channel_id=1, source_target_pairs={{1,0},{2,1},{3,2},{5,4},{6,5},{7,6},{9,8},{10,9},{11,10},{13,12},{... | collective-permute-start | bytes 9224 | tf_op jit(solution)/shard_map/while/body/eval_jaxpr/ppermute | solution.py:21
  1475.9 5.5 collective-permute-start.5
  1485.2 8.2 copy-start.7
  1501.3 209.2 %collective-permute-start.6 = (f32[6,1,128]{1,2,0:T(8,128)}, f32[6,1,128]{1,2,0:T(8,128)}, u32[]{:S(2)}, u32[]{:S(2)}) collective-permute-start(f32[6,1,128]{1,2,0:T(8,128)} %get-tuple-element.913), channel_id=1, source_target_pairs={{0,1},{1,2},{2,3},{4,5},{5,6},{6,7},{8,9},{9,10},{10,11},{12,13},{... | collective-permute-start | bytes 9224 | tf_op jit(solution)/shard_map/while/body/eval_jaxpr/ppermute | solution.py:20
  1512.5 190.6 %collective-permute-start.4 = (f32[6,768,1]{1,2,0:T(1,128)S(1)}, f32[6,768,1]{1,2,0:T(1,128)S(1)}, u32[]{:S(2)}, u32[]{:S(2)}) collective-permute-start(f32[6,768,1]{1,2,0:T(1,128)S(1)} %fusion.112), channel_id=1, source_target_pairs={{0,4},{4,8},{8,12},{12,16},{16,20},{20,24},{24,28},{28,32},{32,36}... | collective-permute-start | bytes 55304 | tf_op jit(solution)/shard_map/while/body/eval_jaxpr/ppermute | solution.py:20
  1513.9 199.8 %collective-permute-start.7 = (f32[6,1,128]{1,2,0:T(8,128)}, f32[6,1,128]{1,2,0:T(8,128)}, u32[]{:S(2)}, u32[]{:S(2)}) collective-permute-start(f32[6,1,128]{1,2,0:T(8,128)} %get-tuple-element.915), channel_id=1, source_target_pairs={{1,0},{2,1},{3,2},{5,4},{6,5},{7,6},{9,8},{10,9},{11,10},{13,12},{... | collective-permute-start | bytes 9224 | tf_op jit(solution)/shard_map/while/body/eval_jaxpr/ppermute | solution.py:21
  1703.3 4.6 collective-permute-start.5
  1727.8 208.0 %collective-permute-start.6 = (f32[6,1,128]{1,2,0:T(8,128)}, f32[6,1,128]{1,2,0:T(8,128)}, u32[]{:S(2)}, u32[]{:S(2)}) collective-permute-start(f32[6,1,128]{1,2,0:T(8,128)} %get-tuple-element.913), channel_id=1, source_target_pairs={{0,1},{1,2},{2,3},{4,5},{5,6},{6,7},{8,9},{9,10},{10,11},{12,13},{... | collective-permute-start | bytes 9224 | tf_op jit(solution)/shard_map/while/body/eval_jaxpr/ppermute | solution.py:20
  1739.3 189.2 %collective-permute-start.4 = (f32[6,768,1]{1,2,0:T(1,128)S(1)}, f32[6,768,1]{1,2,0:T(1,128)S(1)}, u32[]{:S(2)}, u32[]{:S(2)}) collective-permute-start(f32[6,768,1]{1,2,0:T(1,128)S(1)} %fusion.112), channel_id=1, source_target_pairs={{0,4},{4,8},{8,12},{12,16},{16,20},{20,24},{24,28},{28,32},{32,36}... | collective-permute-start | bytes 55304 | tf_op jit(solution)/shard_map/while/body/eval_jaxpr/ppermute | solution.py:20
  1740.6 198.4 %collective-permute-start.7 = (f32[6,1,128]{1,2,0:T(8,128)}, f32[6,1,128]{1,2,0:T(8,128)}, u32[]{:S(2)}, u32[]{:S(2)}) collective-permute-start(f32[6,1,128]{1,2,0:T(8,128)} %get-tuple-element.915), channel_id=1, source_target_pairs={{1,0},{2,1},{3,2},{5,4},{6,5},{7,6},{9,8},{10,9},{11,10},{13,12},{... | collective-permute-start | bytes 9224 | tf_op jit(solution)/shard_map/while/body/eval_jaxpr/ppermute | solution.py:21
  1928.6 4.6 collective-permute-start.5
  1953.1 207.8 %collective-permute-start.6 = (f32[6,1,128]{1,2,0:T(8,128)}, f32[6,1,128]{1,2,0:T(8,128)}, u32[]{:S(2)}, u32[]{:S(2)}) collective-permute-start(f32[6,1,128]{1,2,0:T(8,128)} %get-tuple-element.913), channel_id=1, source_target_pairs={{0,1},{1,2},{2,3},{4,5},{5,6},{6,7},{8,9},{9,10},{10,11},{12,13},{... | collective-permute-start | bytes 9224 | tf_op jit(solution)/shard_map/while/body/eval_jaxpr/ppermute | solution.py:20
  1965.5 188.0 %collective-permute-start.4 = (f32[6,768,1]{1,2,0:T(1,128)S(1)}, f32[6,768,1]{1,2,0:T(1,128)S(1)}, u32[]{:S(2)}, u32[]{:S(2)}) collective-permute-start(f32[6,768,1]{1,2,0:T(1,128)S(1)} %fusion.112), channel_id=1, source_target_pairs={{0,4},{4,8},{8,12},{12,16},{16,20},{20,24},{24,28},{28,32},{32,36}... | collective-permute-start | bytes 55304 | tf_op jit(solution)/shard_map/while/body/eval_jaxpr/ppermute | solution.py:20
  1966.9 197.2 %collective-permute-start.7 = (f32[6,1,128]{1,2,0:T(8,128)}, f32[6,1,128]{1,2,0:T(8,128)}, u32[]{:S(2)}, u32[]{:S(2)}) collective-permute-start(f32[6,1,128]{1,2,0:T(8,128)} %get-tuple-element.915), channel_id=1, source_target_pairs={{1,0},{2,1},{3,2},{5,4},{6,5},{7,6},{9,8},{10,9},{11,10},{13,12},{... | collective-permute-start | bytes 9224 | tf_op jit(solution)/shard_map/while/body/eval_jaxpr/ppermute | solution.py:21
  2153.7 4.6 collective-permute-start.5
  (56 other events, 119.9 us)
where the time goes:
time: 2190 us; the launch traced here: 2180 us
  blocking collectives  1440 us (66%)
  other arithmetic  285 us (13%)
  local copies, waits for them, and re-layouts  241 us (11%)
  starting transfers between devices  208 us (9%)
    all_gather x12, blocking collectives, fold_row(): whole = lax.all_gather(top_row, 'lon', axis=1, tiled=True)  1440 us
    ppermute x24, starting transfers between devices, padded_2(): before = lax.ppermute(last, axis, up)  118 us
    ppermute x24, starting transfers between devices, padded_2(): after = lax.ppermute(first, axis, down)  89.5 us
    rev x12, local copies, waits for them, and re-layouts, fold_row(): flipped = whole[:, ::-1]  77.3 us
    unnamed x5, other arithmetic  58.4 us
    while x168, local copies, waits for them, and re-layouts  53.7 us
    all_gather x6, other arithmetic, fold_row(): whole = lax.all_gather(top_row, 'lon', axis=1, tiled=True)  47.3 us
  transfers between devices with their start and end apart: 48, of which 0 were waited for; matrix products, arithmetic and copies ran while one was open for 13% of the time, Pallas kernels for 0%

commit v1 on v0

v1 whole, which is shorter than its diff:
```python
import functools

import jax
import jax.numpy as jnp
from jax import lax
from jax.experimental import pallas as pl
from jax.experimental.pallas import tpu as pltpu
from jax.sharding import PartitionSpec as P

ITERS = 6
SLABS = 7
PAD = 8
MESH = pl.DeviceIdType.MESH


def exchange_kernel(
    init_ref, drag_ref, dir_ref, mask_ref, cells_ref, sign_ref,
    t_ref, w_ref,
    nat, flip, acc, fold_acc, send_sem, recv_sem,
):
    rows, cols = drag_ref.shape
    ext = cols + 2 * PAD
    n_lon, n_lat = lax.axis_size("lon"), lax.axis_size("lat")
    lon, lat = lax.axis_index("lon"), lax.axis_index("lat")
    top = lat == n_lat - 1
    east, west = lax.rem(lon + 1, n_lon), lax.rem(lon + n_lon - 1, n_lon)

    def device(lon_at, lat_at):
        return {"lon": lon_at, "lat": lat_at}

    barrier = pltpu.get_barrier_semaphore()

    def greet(target):
        pl.semaphore_signal(barrier, inc=1, device_id=target, device_id_type=MESH)

    greet(device(east, lat))
    greet(device(west, lat))

    @pl.when(top)
    def _():
        greet(device(n_lon - 1 - lon, lat))

    @pl.when(jnp.logical_not(top))
    def _():
        greet(device(lon, lat + 1))

    @pl.when(lat > 0)
    def _():
        greet(device(lon, lat - 1))

    def prepare(part, carry):
        here = pl.ds(pl.multiple_of(part * 64, 64), 64)
        there = pl.ds(pl.multiple_of(part * 64 + PAD, 8), 64)
        ocean = mask_ref[here, :].astype(jnp.float32)
        inverse = 1.0 / (1.0 + drag_ref[here, :])
        nat[0, there, :] = init_ref[0, here, :] * (0.2 * ocean)
        nat[1, there, :] = init_ref[1, here, :] * ocean
        nat[2, there, :] = init_ref[2, here, :] * ocean
        nat[3, there, :] = ocean * inverse
        nat[4, there, :] = -(dir_ref[here, :] * inverse)
        return carry

    lax.fori_loop(0, rows // 64, prepare, 0)
    tail = rows + 2 * PAD
    for f in range(5):
        nat[f, tail:, :] = jnp.zeros((nat.shape[1] - tail, cols), jnp.float32)

    lanes = lax.broadcasted_iota(jnp.int32, (PAD, cols), 1)
    for f in range(5):
        tile = nat[f, rows : rows + PAD, :]
        turned = jnp.take_along_axis(tile, cols - 1 - lanes, axis=1)
        if f in (1, 2):
            turned = -turned
        for k in range(PAD):
            flip[f, k : k + 1, :] = turned[PAD - 1 - k : PAD - k, :]

    south_halo, north_halo = pl.ds(0, PAD), pl.ds(rows + PAD, PAD)

    def copy(src, dst, which, slot, target):
        return pltpu.make_async_remote_copy(
            src_ref=src, dst_ref=dst, send_sem=send_sem.at[which],
            recv_sem=recv_sem.at[slot], device_id=target, device_id_type=MESH,
        )

    fold_copy = copy(flip, nat.at[:, north_halo, :], 0, 1, device(n_lon - 1 - lon, lat))
    north_copy = copy(
        nat.at[:, pl.ds(rows, PAD), :], nat.at[:, south_halo, :], 0, 0, device(lon, lat + 1)
    )
    south_copy = copy(
        nat.at[:, pl.ds(PAD, PAD), :], nat.at[:, north_halo, :], 1, 1, device(lon, lat - 1)
    )
    east_copy = copy(
        t_ref.at[:, :, pl.ds(cols, PAD), :], t_ref.at[:, :, pl.ds(0, PAD), :],
        2, 2, device(east, lat),
    )
    west_copy = copy(
        t_ref.at[:, :, pl.ds(PAD, PAD), :], t_ref.at[:, :, pl.ds(cols + PAD, PAD), :],
        3, 3, device(west, lat),
    )

    pl.semaphore_wait(barrier, jnp.where(lat > 0, 4, 3))

    @pl.when(top)
    def _():
        fold_copy.start()

    @pl.when(jnp.logical_not(top))
    def _():
        north_copy.start()

    @pl.when(lat > 0)
    def _():
        south_copy.start()

    @pl.when(lat == 0)
    def _():
        for f in range(5):
            nat[f, 0:PAD, :] = jnp.zeros((PAD, cols), jnp.float32)

    total = cols * n_lon
    chunk = cells_ref.shape[1]
    low = (SLABS + 1) // 2
    a_iota = lax.broadcasted_iota(jnp.int32, (2 * ext, chunk), 0)
    b_iota = lax.broadcasted_iota(jnp.int32, (low * 128, chunk), 0)
    f_iota = lax.broadcasted_iota(jnp.int32, (16, chunk), 0)
    contract = (((1,), (1,)), ((), ()))
    acc[...] = jnp.zeros_like(acc)
    fold_acc[...] = jnp.zeros_like(fold_acc)

    def gather_weights(part, carry):
        cell = cells_ref[pl.ds(part, 1), :]
        sign = sign_ref[pl.ds(part, 1), :].astype(jnp.float32)
        row, col = lax.div(cell, total), lax.rem(cell, total)
        r = row - lat * rows + PAD
        lane = lax.shift_right_arithmetic(r * 9363, 16)
        slab = r - lane * SLABS
        c = col - lon * cols + PAD
        c = jnp.where(c < 0, c + total, c)
        c = jnp.where(c >= total, c - total, c)
        in_rows = (r >= 0) & (r < rows + 2 * PAD)
        a_at = jnp.where(c < ext, (slab // low) * ext + c, -1)
        b_at = jnp.where(in_rows, (slab % low) * 128 + lane, -1)
        a = jnp.where(a_iota == a_at, 1.0, 0.0).astype(jnp.bfloat16)
        b = jnp.where(b_iota == b_at, sign, 0.0).astype(jnp.bfloat16)
        acc[...] += lax.dot_general(a, b, contract, preferred_element_type=jnp.float32)
        fr = 2 * rows - 1 - (row - lat * rows) - rows
        fr = jnp.where(top, fr, -1)
        fc = total - 1 - col - lon * cols + PAD
        fc = jnp.where(fc < 0, fc + total, fc)
        fc = jnp.where(fc >= total, fc - total, fc)
        fa = jnp.where(a_iota[:ext] == fc, 1.0, 0.0).astype(jnp.bfloat16)
        fb = jnp.where((f_iota == fr) & (f_iota < PAD), -sign, 0.0).astype(jnp.bfloat16)
        fold_acc[:, 0:16] += lax.dot_general(
            fa, fb, contract, preferred_element_type=jnp.float32
        )
        return carry

    parts = cells_ref.shape[0]
    lax.fori_loop(0, parts // 2, gather_weights, 0)

    @pl.when(lat > 0)
    def _():
        north_copy.wait_recv()

    south_copy.wait_recv()

    for f in range(5):
        for j in range(SLABS):
            t_ref[f, j, PAD : cols + PAD, :] = nat[f, pl.ds(j, 128, stride=SLABS), :].T
    east_copy.start()
    west_copy.start()

    lax.fori_loop(parts // 2, parts, gather_weights, 0)
    column = lax.broadcasted_iota(jnp.int32, (ext, 128), 1)
    ghosts = fold_acc[...]
    for j in range(SLABS):
        hi, lo = divmod(j, low)
        found = acc[hi * ext : (hi + 1) * ext, lo * 128 : (lo + 1) * 128]
        for k in range(PAD):
            lane, slab = divmod(rows + PAD + k, SLABS)
            if slab == j:
                found += jnp.where(column == lane, pltpu.roll(ghosts, lane - k, 1), 0.0)
        w_ref[j] = found

    east_copy.wait_recv()
    west_copy.wait_recv()
    east_copy.wait_send()
    west_copy.wait_send()
    north_copy.wait_send()

    @pl.when(lat > 0)
    def _():
        south_copy.wait_send()


def chain_kernel(
    t_ref, w_ref, curv_ref, state_ref, tangent_ref, levels, back, curv, nat
):
    cols = t_ref.shape[2] - 2 * PAD
    rows = curv_ref.shape[0]
    tiles = t_ref.shape[2] // 8

    def rows_at(i, shift=0):
        return pl.ds(PAD + 8 * i + shift, 8)

    def step(src, dst, i, spin):
        here = pl.ds(8 * i, 8)
        damp = [t_ref[3, j, here, :] for j in range(SLABS)]
        factor = [t_ref[4, j, here, :] for j in range(SLABS)]
        scale = [jnp.where(d > 0.0, 0.04, 0.0) for d in damp]
        new = [[], []]
        for part in range(2):
            h, u, v = 3 * part, 3 * part + 1, 3 * part + 2
            hs = [src[h, j, rows_at(i), :] for j in range(SLABS)]
            vs = [src[v, j, rows_at(i), :] for j in range(SLABS)]
            h_up, h_down = pltpu.roll(hs[0], 127, 1), pltpu.roll(hs[-1], 1, 1)
            v_up, v_down = pltpu.roll(vs[0], 127, 1), pltpu.roll(vs[-1], 1, 1)
            for j in range(SLABS):
                north_h = hs[j + 1] if j < SLABS - 1 else h_up
                south_h = hs[j - 1] if j > 0 else h_down
                north_v = vs[j + 1] if j < SLABS - 1 else v_up
                south_v = vs[j - 1] if j > 0 else v_down
                um = src[u, j, rows_at(i), :]
                du = src[u, j, rows_at(i, 1), :] - src[u, j, rows_at(i, -1), :]
                dh = src[h, j, rows_at(i, 1), :] - src[h, j, rows_at(i, -1), :]
                new_h = hs[j] - scale[j] * (du + (north_v - south_v))
                new_u = (um - dh + spin * vs[j]) * damp[j]
                new_v = (vs[j] - (north_h - south_h) - spin * um) * damp[j]
                if part == 1:
                    new_u += factor[j] * new[0][j][0]
                    new_v += factor[j] * new[0][j][1]
                dst[h, j, rows_at(i), :] = new_h
                dst[u, j, rows_at(i), :] = new_u
                dst[v, j, rows_at(i), :] = new_v
                new[part].append((new_u, new_v))
        return new

    zero = jnp.zeros((8, 128), jnp.float32)
    for field in range(6):
        for j in range(SLABS):
            for n in range(ITERS + 1):
                levels[n, field, j, 0:PAD, :] = zero
                levels[n, field, j, cols + 3 * PAD :, :] = zero
            for n in range(2):
                back[n, field, j, 0:PAD, :] = zero
                back[n, field, j, cols + 3 * PAD :, :] = zero

    def start(i, carry):
        for j in range(SLABS):
            for field in range(3):
                levels[0, field, j, rows_at(i), :] = t_ref[field, j, pl.ds(8 * i, 8), :]
                levels[0, 3 + field, j, rows_at(i), :] = zero
            weight = t_ref[3, j, pl.ds(8 * i, 8), :] * w_ref[j, pl.ds(8 * i, 8), :]
            for field in (0, 1, 3, 4):
                back[0, field, j, rows_at(i), :] = zero
            back[0, 2, j, rows_at(i), :] = weight
            back[0, 5, j, rows_at(i), :] = weight * t_ref[4, j, pl.ds(8 * i, 8), :]
        return carry

    lax.fori_loop(0, tiles, start, 0)

    def forward(n, carry):
        for i in range(tiles):
            step(levels.at[n], levels.at[n + 1], i, 0.25)
        return carry

    lax.fori_loop(0, ITERS, forward, 0)

    for out, first in ((state_ref, 0), (tangent_ref, 3)):
        for field in range(3):
            for j in range(SLABS):
                block = levels[ITERS, first + field, j, 2 * PAD : 2 * PAD + cols, :].T
                if field == 0:
                    block = block * 5.0
                nat[first + field, pl.ds(j, 128, stride=SLABS), :] = block
            out[field] = nat[first + field, PAD : PAD + rows, :]

    for i in range(1, tiles - 1):
        for j in range(SLABS):
            at = rows_at(i)
            curv[j, pl.ds(8 * i - 8, 8), :] = -(
                levels[ITERS, 5, j, at, :] * back[0, 2, j, at, :]
                + levels[ITERS, 2, j, at, :] * back[0, 5, j, at, :]
            )

    def backward(k, carry):
        src, dst = back.at[lax.rem(k, 2)], back.at[lax.rem(k + 1, 2)]
        level = levels.at[ITERS - 1 - k]
        for i in range(tiles):
            new = step(src, dst, i, -0.25)
            if 0 < i < tiles - 1:
                for j in range(SLABS):
                    at, own = rows_at(i), pl.ds(8 * i - 8, 8)
                    (qu, qv), (ru, rv) = new[0][j], new[1][j]
                    curv[j, own, :] -= (
                        levels_uv(level, 4, j, at) * qu + levels_uv(level, 5, j, at) * qv
                    ) + (levels_uv(level, 1, j, at) * ru + levels_uv(level, 2, j, at) * rv)
        return carry

    def levels_uv(level, field, j, at):
        return level[field, j, at, :]

    lax.fori_loop(0, ITERS - 1, backward, 0)
    for j in range(SLABS):
        nat[6, pl.ds(j, 128, stride=SLABS), :] = curv[j].T
    curv_ref[...] = nat[6, PAD : PAD + rows, :]


def on_device(initial_state, bottom_drag, drag_direction, land_mask, section_cells, section_sign):
    rows, cols = bottom_drag.shape
    ext = cols + 2 * PAD
    f32 = jnp.float32
    vmem = pl.BlockSpec(memory_space=pltpu.VMEM)
    chunk = 512
    fields, weights = pl.pallas_call(
        exchange_kernel,
        out_shape=(
            jax.ShapeDtypeStruct((5, SLABS, ext, 128), f32),
            jax.ShapeDtypeStruct((SLABS, ext, 128), f32),
        ),
        in_specs=[vmem] * 6,
        out_specs=(vmem, vmem),
        scratch_shapes=[
            pltpu.VMEM((5, SLABS * 128, cols), f32),
            pltpu.VMEM((5, PAD, cols), f32),
            pltpu.VMEM((2 * ext, (SLABS + 1) // 2 * 128), f32),
            pltpu.VMEM((ext, 128), f32),
            pltpu.SemaphoreType.DMA((4,)),
            pltpu.SemaphoreType.DMA((4,)),
        ],
        compiler_params=pltpu.CompilerParams(
            collective_id=0, has_side_effects=True, vmem_limit_bytes=40 * 1024 * 1024
        ),
        name="exchange",
    )(
        initial_state, bottom_drag, drag_direction, land_mask,
        section_cells.reshape(-1, chunk), section_sign.reshape(-1, chunk),
    )
    return pl.pallas_call(
        chain_kernel,
        out_shape=(
            jax.ShapeDtypeStruct((rows, cols), f32),
            jax.ShapeDtypeStruct((3, rows, cols), f32),
            jax.ShapeDtypeStruct((3, rows, cols), f32),
        ),
        in_specs=[vmem] * 2,
        out_specs=(vmem, vmem, vmem),
        scratch_shapes=[
            pltpu.VMEM((ITERS + 1, 6, SLABS, ext + 2 * PAD, 128), f32),
            pltpu.VMEM((2, 6, SLABS, ext + 2 * PAD, 128), f32),
            pltpu.VMEM((SLABS, cols, 128), f32),
            pltpu.VMEM((7, SLABS * 128, cols), f32),
        ],
        compiler_params=pltpu.CompilerParams(vmem_limit_bytes=56 * 1024 * 1024),
        name="chain",
    )(fields, weights)


def solution(mesh):
    return jax.shard_map(
        on_device,
        mesh=mesh,
        in_specs=(
            P(None, "lat", "lon"),
            P("lat", "lon"),
            P("lat", "lon"),
            P("lat", "lon"),
            P(),
            P(),
        ),
        out_specs=(P("lat", "lon"), P(None, "lat", "lon"), P(None, "lat", "lon")),
        check_vma=False,
    )
```

time: 2190 us -> 47.6 us (0.02)
  blocking collectives: 1440 us -> 0 us
  other arithmetic: 285 us -> 0 us
  local copies, waits for them, and re-layouts: 241 us -> 8.07 us
  starting transfers between devices: 208 us -> 0 us
  Pallas kernels: 0 us -> 38.5 us
    all_gather x12 -> x0, blocking collectives: 1440 us -> none  [fold_row(): whole = lax.all_gather(top_row, 'lon', axis=1, tiled=True)]
    ppermute x48 -> x0, starting transfers between devices: 208 us -> none  [the longest x24 118 us: padded_2(): before = lax.ppermute(last, axis, up)]
    rev x12 -> x0, local copies, waits for them, and re-layouts: 77.3 us -> none  [fold_row(): flipped = whole[:, ::-1]]
    scatter-add x30 -> x0, local copies, waits for them, and re-layouts: 61.4 us -> none  [the longest x6 14.5 us: pad_back(): inner = inner.at[:, -1, :].add(edge_got[:, 3, :])]
    unnamed x5 -> x0, other arithmetic: 58.4 us -> none
    while x168 -> x0, local copies, waits for them, and re-layouts: 53.7 us -> none
    all_gather x6 -> x0, other arithmetic: 47.3 us -> none  [fold_row(): whole = lax.all_gather(top_row, 'lon', axis=1, tiled=True)]
    pallas_call x0 -> x2, Pallas kernels: none -> 38.5 us  [the longest x1 21.4 us: on_device(): pl.pallas_call(chain_kernel, out_shape=(jax.ShapeDtypeStruct((rows, cols)...]
  transfers between devices with their start and end apart: 48 -> 0, of which waited for: 0 -> 0; matrix products, arithmetic and copies ran while one was open for 13% -> 0% of each run, Pallas kernels for 0% -> 0%
where the time goes in v1:
time: 47.6 us; the launch traced here: 47.2 us
  Pallas kernels  38.5 us (81%)
  local copies, waits for them, and re-layouts  8.07 us (17%)
  between operations  0.65 us (1%)
    pallas_call x1, Pallas kernels, on_device(): pl.pallas_call(chain_kernel, out_shape=(jax.ShapeDtypeStruct((rows, cols)...  21.4 us
    pallas_call x1, Pallas kernels, on_device(): pl.pallas_call(exchange_kernel, out_shape=(jax.ShapeDtypeStruct((5, SLABS...  17 us
    unnamed x12, local copies, waits for them, and re-layouts  6.54 us

profile of v1, /device:TPU:1, one launch (start us, length us, event | category | flops | bytes accessed | tf_op | source)
XLA Modules:
  0.0 47.2 jit_solution(16232728926716343215)
XLA Ops:
  0.6 0.8 %reshape.12.cells_ref = s32[16,512]{1,0:T(8,128)S(1)} reshape(s32[8192]{0:T(1024)} %param.10) | data formatting | bytes 65536 | tf_op jit(solution)/shard_map/reshape | solution.py:337
  1.4 0.8 %reshape.13.sign_ref = s32[16,512]{1,0:T(8,128)S(1)} reshape(s32[8192]{0:T(1024)} %param.11) | data formatting | bytes 65536 | tf_op jit(solution)/shard_map/reshape | solution.py:337
  2.2 0.0 copy-start.1
  2.2 1.3 %copy-done.1 = f32[3,768,128]{2,1,0:T(8,128)S(1)} copy-done((f32[3,768,128]{2,1,0:T(8,128)S(1)}, f32[3,768,128]{2,1,0:T(8,128)}, u32[]{:S(2)}) %copy-start.1) | copy-done | bytes 1179672
  3.4 0.0 copy-start.3
  3.4 1.0 %copy-done.3 = f32[768,128]{1,0:T(8,128)S(1)} copy-done((f32[768,128]{1,0:T(8,128)S(1)}, f32[768,128]{1,0:T(8,128)}, u32[]{:S(2)}) %copy-start.3) | copy-done | bytes 393240
  4.4 0.0 copy-start.4
  4.4 1.0 %copy-done.4 = f32[768,128]{1,0:T(8,128)S(1)} copy-done((f32[768,128]{1,0:T(8,128)S(1)}, f32[768,128]{1,0:T(8,128)}, u32[]{:S(2)}) %copy-start.4) | copy-done | bytes 393240
  5.4 0.0 copy-start.5
  5.4 1.0 %copy-done.5 = s32[768,128]{1,0:T(8,128)S(1)} copy-done((s32[768,128]{1,0:T(8,128)S(1)}, s32[768,128]{1,0:T(8,128)}, u32[]{:S(2)}) %copy-start.5) | copy-done | bytes 393240
  6.4 17.0 %exchange.1 = (f32[5,7,144,128]{3,2,1,0:T(8,128)S(1)}, f32[7,144,128]{2,1,0:T(8,128)S(1)}) custom-call(f32[3,768,128]{2,1,0:T(8,128)S(1)} %copy-done.1, f32[768,128]{1,0:T(8,128)S(1)} %copy-done.3, f32[768,128]{1,0:T(8,128)S(1)} %copy-done.4, s32[768,128]{1,0:T(8,128)S(1)} %copy-done.5, s32[16,512]{1,0:T(8,128)S(1)} %reshape.12.cells_ref, ...), custom_call_target="tpu_custom_call" | custom-call | tf_op jit(solution)/shard_map/exchange/pallas_call | solution.py:315
  23.5 0.0 copy-start
  23.5 1.5 %copy-done = f32[5,7,144,128]{3,2,1,0:T(8,128)} copy-done((f32[5,7,144,128]{3,2,1,0:T(8,128)}, f32[5,7,144,128]{3,2,1,0:T(8,128)S(1)}, u32[]{:S(2)}) %copy-start) | copy-done | bytes 2580504
  25.0 0.0 copy-start.2
  25.0 0.8 %copy-done.2 = f32[7,144,128]{2,1,0:T(8,128)} copy-done((f32[7,144,128]{2,1,0:T(8,128)}, f32[7,144,128]{2,1,0:T(8,128)S(1)}, u32[]{:S(2)}) %copy-start.2) | copy-done | bytes 516120
  25.8 21.4 %chain.1 = (f32[768,128]{1,0:T(8,128)}, f32[3,768,128]{2,1,0:T(8,128)}, f32[3,768,128]{2,1,0:T(8,128)}) custom-call(f32[5,7,144,128]{3,2,1,0:T(8,128)} %copy-done, f32[7,144,128]{2,1,0:T(8,128)} %copy-done.2), custom_call_target="tpu_custom_call" | custom-call | tf_op jit(solution)/shard_map/chain/pallas_call | solution.py:339
Async XLA Ops:
  2.2 1.3 %copy-start.1 = (f32[3,768,128]{2,1,0:T(8,128)S(1)}, f32[3,768,128]{2,1,0:T(8,128)}, u32[]{:S(2)}) copy-start(f32[3,768,128]{2,1,0:T(8,128)} %init_ref.1) | copy-start | bytes 3538948
  3.4 1.0 %copy-start.3 = (f32[768,128]{1,0:T(8,128)S(1)}, f32[768,128]{1,0:T(8,128)}, u32[]{:S(2)}) copy-start(f32[768,128]{1,0:T(8,128)} %drag_ref.1) | copy-start | bytes 1179652
  4.4 1.0 %copy-start.4 = (f32[768,128]{1,0:T(8,128)S(1)}, f32[768,128]{1,0:T(8,128)}, u32[]{:S(2)}) copy-start(f32[768,128]{1,0:T(8,128)} %dir_ref.1) | copy-start | bytes 1179652
  5.4 1.0 %copy-start.5 = (s32[768,128]{1,0:T(8,128)S(1)}, s32[768,128]{1,0:T(8,128)}, u32[]{:S(2)}) copy-start(s32[768,128]{1,0:T(8,128)} %mask_ref.1) | copy-start | bytes 1179652
  23.5 1.5 %copy-start = (f32[5,7,144,128]{3,2,1,0:T(8,128)}, f32[5,7,144,128]{3,2,1,0:T(8,128)S(1)}, u32[]{:S(2)}) copy-start(f32[5,7,144,128]{3,2,1,0:T(8,128)S(1)} %get-tuple-element.5.t_ref) | copy-start | bytes 7741444
  25.0 0.8 %copy-start.2 = (f32[7,144,128]{2,1,0:T(8,128)}, f32[7,144,128]{2,1,0:T(8,128)S(1)}, u32[]{:S(2)}) copy-start(f32[7,144,128]{2,1,0:T(8,128)S(1)} %get-tuple-element.6.w_ref) | copy-start | bytes 1548292

commit v2 on v1

v2 whole, which is shorter than its diff:
```python
import functools

import jax
import jax.numpy as jnp
from jax import lax
from jax.experimental import pallas as pl
from jax.experimental.pallas import tpu as pltpu
from jax.sharding import PartitionSpec as P

ITERS = 6
SLABS = 7
LOW = (SLABS + 1) // 2
PAD = 8
CHUNK = 8
MESH = pl.DeviceIdType.MESH


def exchange_kernel(
    init_hbm, drag_hbm, dir_hbm, mask_hbm, cells_hbm, sign_hbm,
    t_hbm, w_hbm,
    t_ref, w_ref, init_ref, drag_ref, dir_ref, mask_ref, cells_ref, sign_ref,
    nat, flip, at_ref, acc, fold_acc, load_sem, send_sem, recv_sem, out_sem,
):
    rows, cols = drag_ref.shape
    ext = cols + 2 * PAD
    n_lon, n_lat = lax.axis_size("lon"), lax.axis_size("lat")
    lon, lat = lax.axis_index("lon"), lax.axis_index("lat")
    top = lat == n_lat - 1
    east, west = lax.rem(lon + 1, n_lon), lax.rem(lon + n_lon - 1, n_lon)

    loads = [
        pltpu.make_async_copy(src, dst, load_sem.at[k])
        for k, (src, dst) in enumerate((
            (mask_hbm, mask_ref), (drag_hbm, drag_ref), (init_hbm, init_ref),
            (dir_hbm, dir_ref), (cells_hbm, cells_ref), (sign_hbm, sign_ref),
        ))
    ]
    for load in loads:
        load.start()

    def device(lon_at, lat_at):
        return {"lon": lon_at, "lat": lat_at}

    barrier = pltpu.get_barrier_semaphore()

    def greet(target):
        pl.semaphore_signal(barrier, inc=1, device_id=target, device_id_type=MESH)

    greet(device(east, lat))
    greet(device(west, lat))

    @pl.when(top)
    def _():
        greet(device(n_lon - 1 - lon, lat))

    @pl.when(jnp.logical_not(top))
    def _():
        greet(device(lon, lat + 1))

    @pl.when(lat > 0)
    def _():
        greet(device(lon, lat - 1))

    def prepare(part, carry):
        here = pl.ds(pl.multiple_of(part * 64, 64), 64)
        there = pl.ds(pl.multiple_of(part * 64 + PAD, 8), 64)
        ocean = mask_ref[here, :].astype(jnp.float32)
        inverse = 1.0 / (1.0 + drag_ref[here, :])
        nat[0, there, :] = init_ref[0, here, :] * (0.2 * ocean)
        nat[1, there, :] = init_ref[1, here, :] * ocean
        nat[2, there, :] = init_ref[2, here, :] * ocean
        nat[3, there, :] = ocean * inverse
        nat[4, there, :] = -(dir_ref[here, :] * inverse)
        return carry

    tail = rows + 2 * PAD
    for f in range(5):
        nat[f, tail:, :] = jnp.zeros((nat.shape[1] - tail, cols), jnp.float32)
    for load in loads:
        load.wait()
    lax.fori_loop(0, rows // 64, prepare, 0)

    lanes = lax.broadcasted_iota(jnp.int32, (PAD, cols), 1)
    for f in range(5):
        tile = nat[f, rows : rows + PAD, :]
        turned = jnp.take_along_axis(tile, cols - 1 - lanes, axis=1)
        if f in (1, 2):
            turned = -turned
        for k in range(PAD):
            flip[f, k : k + 1, :] = turned[PAD - 1 - k : PAD - k, :]

    south_halo, north_halo = pl.ds(0, PAD), pl.ds(rows + PAD, PAD)

    def copy(src, dst, which, slot, target):
        return pltpu.make_async_remote_copy(
            src_ref=src, dst_ref=dst, send_sem=send_sem.at[which],
            recv_sem=recv_sem.at[slot], device_id=target, device_id_type=MESH,
        )

    fold_copy = copy(flip, nat.at[:, north_halo, :], 0, 1, device(n_lon - 1 - lon, lat))
    north_copy = copy(
        nat.at[:, pl.ds(rows, PAD), :], nat.at[:, south_halo, :], 0, 0, device(lon, lat + 1)
    )
    south_copy = copy(
        nat.at[:, pl.ds(PAD, PAD), :], nat.at[:, north_halo, :], 1, 1, device(lon, lat - 1)
    )
    east_copy = copy(
        t_ref.at[:, :, pl.ds(cols, PAD), :], t_ref.at[:, :, pl.ds(0, PAD), :],
        2, 2, device(east, lat),
    )
    west_copy = copy(
        t_ref.at[:, :, pl.ds(PAD, PAD), :], t_ref.at[:, :, pl.ds(cols + PAD, PAD), :],
        3, 3, device(west, lat),
    )

    pl.semaphore_wait(barrier, jnp.where(lat > 0, 4, 3))

    @pl.when(top)
    def _():
        fold_copy.start()

    @pl.when(jnp.logical_not(top))
    def _():
        north_copy.start()

    @pl.when(lat > 0)
    def _():
        south_copy.start()

    @pl.when(lat == 0)
    def _():
        for f in range(5):
            nat[f, 0:PAD, :] = jnp.zeros((PAD, cols), jnp.float32)

    total = cols * n_lon
    cell = cells_ref[...]
    row, col = lax.div(cell, total), lax.rem(cell, total)
    r = row - lat * rows + PAD
    lane = lax.shift_right_arithmetic(r * 9363, 16)
    slab = r - lane * SLABS
    c = col - lon * cols + PAD
    c = jnp.where(c < 0, c + total, c)
    c = jnp.where(c >= total, c - total, c)
    in_rows = (r >= 0) & (r < rows + 2 * PAD)
    at_ref[0] = jnp.where(c < ext, lax.div(slab, LOW) * ext + c, -1)
    at_ref[1] = jnp.where(in_rows, lax.rem(slab, LOW) * 128 + lane, -1)
    fr = rows - 1 - (row - lat * rows)
    at_ref[2] = jnp.where(top & (fr < PAD), fr, -1)
    fc = total - 1 - col - lon * cols + PAD
    fc = jnp.where(fc < 0, fc + total, fc)
    at_ref[3] = jnp.where(fc >= total, fc - total, fc)

    contract = (((1,), (1,)), ((), ()))
    acc[...] = jnp.zeros_like(acc)
    fold_acc[...] = jnp.zeros_like(fold_acc)

    def spread(which, at):
        line = at_ref[which, pl.ds(at, 1), :]
        return jnp.broadcast_to(line, (16, 128)).astype(jnp.int16)

    def one_hot(which, first, size, value=None):
        steps = lax.broadcasted_iota(jnp.int16, (size, 128), 0)
        found = []
        for k in range(CHUNK):
            at = jnp.concatenate([spread(which, first + k)] * (size // 16), axis=0)
            if value is None:
                hit = jnp.ones((size, 128), jnp.bfloat16)
            else:
                hit = jnp.concatenate([value[k]] * (size // 16), axis=0)
            found.append(jnp.where(steps == at, hit, jnp.zeros((size, 128), jnp.bfloat16)))
        return jnp.concatenate(found, axis=1)

    def gather_weights(part, carry):
        first = part * CHUNK
        signs = [
            jnp.broadcast_to(sign_ref[pl.ds(first + k, 1), :], (16, 128))
            .astype(jnp.float32).astype(jnp.bfloat16)
            for k in range(CHUNK)
        ]
        a = one_hot(0, first, 2 * ext)
        b = one_hot(1, first, LOW * 128, signs)
        acc[...] += lax.dot_general(a, b, contract, preferred_element_type=jnp.float32)
        fa = one_hot(3, first, ext)
        fb = one_hot(2, first, 16, signs)
        fold_acc[:, 0:16] += lax.dot_general(
            fa, fb, contract, preferred_element_type=jnp.float32
        )
        return carry

    parts = cells_ref.shape[0] // CHUNK
    lax.fori_loop(0, parts // 2, gather_weights, 0)

    @pl.when(lat > 0)
    def _():
        north_copy.wait_recv()

    south_copy.wait_recv()

    for f in range(5):
        for j in range(SLABS):
            t_ref[f, j, PAD : cols + PAD, :] = nat[f, pl.ds(j, 128, stride=SLABS), :].T
    east_copy.start()
    west_copy.start()

    def store(start, size, which):
        part = pl.ds(start, size)
        return pltpu.make_async_copy(
            t_ref.at[:, :, part, :], t_hbm.at[:, :, part, :], out_sem.at[which]
        )

    own_out = store(PAD, cols, 0)
    own_out.start()

    lax.fori_loop(parts // 2, parts, gather_weights, 0)
    column = lax.broadcasted_iota(jnp.int32, (ext, 128), 1)
    ghosts = fold_acc[...]
    for j in range(SLABS):
        hi, lo = divmod(j, LOW)
        found = acc[hi * ext : (hi + 1) * ext, lo * 128 : (lo + 1) * 128]
        for k in range(PAD):
            lane_at, slab_at = divmod(rows + PAD + k, SLABS)
            if slab_at == j:
                turned = pltpu.roll(ghosts, lane_at - k, 1)
                found -= jnp.where(column == lane_at, turned, 0.0)
        w_ref[j] = found
    w_out = pltpu.make_async_copy(w_ref, w_hbm, out_sem.at[1])
    w_out.start()

    east_copy.wait_recv()
    east_out = store(0, PAD, 2)
    east_out.start()
    west_copy.wait_recv()
    west_out = store(cols + PAD, PAD, 3)
    west_out.start()
    east_copy.wait_send()
    west_copy.wait_send()
    north_copy.wait_send()

    @pl.when(lat > 0)
    def _():
        south_copy.wait_send()

    own_out.wait()
    w_out.wait()
    east_out.wait()
    west_out.wait()


def chain_kernel(
    t_hbm, w_hbm, curv_hbm, state_hbm, tangent_hbm,
    t_ref, w_ref, levels, back_a, back_b, scale_ref, curv, nat, load_sem, out_sem,
):
    ext = t_ref.shape[2]
    cols = ext - 2 * PAD
    rows = curv_hbm.shape[0]
    tiles = ext // 8
    third = ext // 3

    loads = [
        pltpu.make_async_copy(
            t_hbm.at[:, :, pl.ds(k * third, third), :],
            t_ref.at[:, :, pl.ds(k * third, third), :], load_sem.at[k],
        )
        for k in range(3)
    ] + [pltpu.make_async_copy(w_hbm, w_ref, load_sem.at[3])]
    for load in loads:
        load.start()

    def around(src, field, j, i):
        if i == 0:
            low = pltpu.roll(src[field, j, 0:8, :], 1, 0)
        else:
            low = src[field, j, 8 * i - 1 : 8 * i + 7, :]
        if i == tiles - 1:
            high = pltpu.roll(src[field, j, 8 * i : 8 * i + 8, :], 7, 0)
        else:
            high = src[field, j, 8 * i + 1 : 8 * i + 9, :]
        return high - low

    def step(src, dst, i, spin, use=None, first=False):
        here = slice(8 * i, 8 * i + 8)
        parts = (0,) if first else (0, 3)

        def get(field, j):
            return src[field, j, here, :]

        up = {f: pltpu.roll(get(f, 0), 127, 1) for p in parts for f in (p, p + 2)}
        before = {f: pltpu.roll(get(f, SLABS - 1), 1, 1) for p in parts for f in (p, p + 2)}
        now = {f: get(f, 0) for p in parts for f in (p, p + 2)}
        for j in range(SLABS):
            damp, factor = t_ref[3, j, here, :], t_ref[4, j, here, :]
            if first:
                scale = jnp.where(damp > 0.0, 0.04, 0.0)
                scale_ref[j, here, :] = scale
            else:
                scale = scale_ref[j, here, :]
            after = {
                f: get(f, j + 1) if j < SLABS - 1 else up[f] for p in parts for f in (p, p + 2)
            }
            new = []
            for p in parts:
                h, u, v = p, p + 1, p + 2
                um, vm = get(u, j), now[v]
                new_h = now[h] - scale * (around(src, u, j, i) + (after[v] - before[v]))
                new_u = (um - around(src, h, j, i) + spin * vm) * damp
                new_v = (vm - (after[h] - before[h]) - spin * um) * damp
                if p:
                    new_u += factor * new[0]
                    new_v += factor * new[1]
                new += [new_u, new_v]
                dst[h, j, here, :] = new_h
                dst[u, j, here, :] = new_u
                dst[v, j, here, :] = new_v
            if first:
                new += [factor * new[0], factor * new[1]]
                dst[3, j, here, :] = jnp.zeros((8, 128), jnp.float32)
                dst[4, j, here, :] = new[2]
                dst[5, j, here, :] = new[3]
            if use is not None:
                use(j, i, here, new)
            before, now = now, after

    def weigh(level):
        def use(j, i, here, new):
            if 0 < i < tiles - 1:
                qu, qv, ru, rv = new
                own = slice(8 * i - 8, 8 * i)
                curv[j, own, :] -= (
                    level[4, j, here, :] * qu + level[5, j, here, :] * qv
                ) + (level[1, j, here, :] * ru + level[2, j, here, :] * rv)
        return use

    def turn(field, times=None):
        for j in range(SLABS):
            block = levels[ITERS - 1, field, j, PAD : PAD + cols, :]
            if times is not None:
                block = block * times
            nat[field, pl.ds(j, 128, stride=SLABS), :] = block.T

    def send(field, out, at):
        return pltpu.make_async_copy(
            nat.at[field, pl.ds(PAD, rows), :], out.at[at], out_sem.at[field]
        )

    ready = 0
    for i in range(tiles):
        while ready < 3 and ready * third < 8 * i + 9:
            loads[ready].wait()
            ready += 1
        step(t_ref, levels.at[0], i, 0.25, first=True)

    def forward(n, carry):
        for i in range(tiles):
            step(levels.at[n], levels.at[n + 1], i, 0.25)
        return carry

    lax.fori_loop(0, ITERS - 1, forward, 0)

    loads[3].wait()
    last, prior = levels.at[ITERS - 1], levels.at[ITERS - 2]
    for i in range(tiles):
        here = slice(8 * i, 8 * i + 8)
        q = [t_ref[3, j, here, :] * w_ref[j, here, :] for j in range(SLABS)]
        r = [t_ref[4, j, here, :] * q[j] for j in range(SLABS)]
        q = [pltpu.roll(q[-1], 1, 1)] + q + [pltpu.roll(q[0], 127, 1)]
        r = [pltpu.roll(r[-1], 1, 1)] + r + [pltpu.roll(r[0], 127, 1)]
        for j in range(SLABS):
            damp, factor = t_ref[3, j, here, :], t_ref[4, j, here, :]
            scale = scale_ref[j, here, :]
            qv, rv = q[j + 1] * damp, r[j + 1] * damp
            qu, ru = -0.25 * qv, -0.25 * rv
            rv, ru = rv + factor * qv, ru + factor * qu
            back_a[0, j, here, :] = scale * (q[j] - q[j + 2])
            back_a[1, j, here, :] = qu
            back_a[2, j, here, :] = qv
            back_a[3, j, here, :] = scale * (r[j] - r[j + 2])
            back_a[4, j, here, :] = ru
            back_a[5, j, here, :] = rv
            if 0 < i < tiles - 1:
                done = last[5, j, here, :] * q[j + 1] + last[2, j, here, :] * r[j + 1]
                done += prior[4, j, here, :] * qu + prior[5, j, here, :] * qv
                done += prior[1, j, here, :] * ru + prior[2, j, here, :] * rv
                curv[j, 8 * i - 8 : 8 * i, :] = -done
    turn(0, 5.0)
    turn(3, 5.0)
    send(0, state_hbm, 0).start()
    send(3, tangent_hbm, 0).start()

    def backward(k, carry):
        turn(1 + k)
        for i in range(tiles):
            step(back_a, back_b, i, -0.25, weigh(levels.at[ITERS - 3 - 2 * k]))
        send(1 + k, state_hbm, 1 + k).start()
        turn(4 + k)
        for i in range(tiles):
            step(back_b, back_a, i, -0.25, weigh(levels.at[ITERS - 4 - 2 * k]))
        send(4 + k, tangent_hbm, 1 + k).start()
        return carry

    lax.fori_loop(0, (ITERS - 2) // 2, backward, 0)
    for j in range(SLABS):
        nat[6, pl.ds(j, 128, stride=SLABS), :] = curv[j].T
    curv_copy = pltpu.make_async_copy(nat.at[6, pl.ds(PAD, rows), :], curv_hbm, out_sem.at[6])
    curv_copy.start()
    for f in range(3):
        send(f, state_hbm, f).wait()
        send(3 + f, tangent_hbm, f).wait()
    curv_copy.wait()


def on_device(initial_state, bottom_drag, drag_direction, land_mask, section_cells, section_sign):
    rows, cols = bottom_drag.shape
    ext = cols + 2 * PAD
    f32, i32 = jnp.float32, jnp.int32
    hbm = pl.BlockSpec(memory_space=pl.ANY)
    lines = section_cells.shape[0] // 128
    fields, weights = pl.pallas_call(
        exchange_kernel,
        out_shape=(
            jax.ShapeDtypeStruct((5, SLABS, ext, 128), f32),
            jax.ShapeDtypeStruct((SLABS, ext, 128), f32),
        ),
        in_specs=[hbm] * 6,
        out_specs=(hbm, hbm),
        scratch_shapes=[
            pltpu.VMEM((5, SLABS, ext, 128), f32),
            pltpu.VMEM((SLABS, ext, 128), f32),
            pltpu.VMEM((3, rows, cols), f32),
            pltpu.VMEM((rows, cols), f32),
            pltpu.VMEM((rows, cols), f32),
            pltpu.VMEM((rows, cols), i32),
            pltpu.VMEM((lines, 128), i32),
            pltpu.VMEM((lines, 128), i32),
            pltpu.VMEM((5, SLABS * 128, cols), f32),
            pltpu.VMEM((5, PAD, cols), f32),
            pltpu.VMEM((4, lines, 128), i32),
            pltpu.VMEM((2 * ext, LOW * 128), f32),
            pltpu.VMEM((ext, 128), f32),
            pltpu.SemaphoreType.DMA((6,)),
            pltpu.SemaphoreType.DMA((4,)),
            pltpu.SemaphoreType.DMA((4,)),
            pltpu.SemaphoreType.DMA((4,)),
        ],
        compiler_params=pltpu.CompilerParams(
            collective_id=0, has_side_effects=True, vmem_limit_bytes=56 * 1024 * 1024
        ),
        name="exchange",
    )(
        initial_state, bottom_drag, drag_direction, land_mask,
        section_cells.reshape(lines, 128), section_sign.reshape(lines, 128),
    )
    return pl.pallas_call(
        chain_kernel,
        out_shape=(
            jax.ShapeDtypeStruct((rows, cols), f32),
            jax.ShapeDtypeStruct((3, rows, cols), f32),
            jax.ShapeDtypeStruct((3, rows, cols), f32),
        ),
        in_specs=[hbm] * 2,
        out_specs=(hbm, hbm, hbm),
        scratch_shapes=[
            pltpu.VMEM((5, SLABS, ext, 128), f32),
            pltpu.VMEM((SLABS, ext, 128), f32),
            pltpu.VMEM((ITERS, 6, SLABS, ext, 128), f32),
            pltpu.VMEM((6, SLABS, ext, 128), f32),
            pltpu.VMEM((6, SLABS, ext, 128), f32),
            pltpu.VMEM((SLABS, ext, 128), f32),
            pltpu.VMEM((SLABS, cols, 128), f32),
            pltpu.VMEM((7, SLABS * 128, cols), f32),
            pltpu.SemaphoreType.DMA((4,)),
            pltpu.SemaphoreType.DMA((7,)),
        ],
        compiler_params=pltpu.CompilerParams(vmem_limit_bytes=56 * 1024 * 1024),
        name="chain",
    )(fields, weights)


def solution(mesh):
    return jax.shard_map(
        on_device,
        mesh=mesh,
        in_specs=(
            P(None, "lat", "lon"),
            P("lat", "lon"),
            P("lat", "lon"),
            P("lat", "lon"),
            P(),
            P(),
        ),
        out_specs=(P("lat", "lon"), P(None, "lat", "lon"), P(None, "lat", "lon")),
        check_vma=False,
    )
```

time: 47.6 us -> 29.5 us (0.62)
  Pallas kernels: 38.5 us -> 28.7 us
  local copies, waits for them, and re-layouts: 8.07 us -> 0 us
    pallas_call x1, Pallas kernels: 21.4 us -> 10.7 us  [on_device(): pl.pallas_call(chain_kernel, out_shape=(jax.ShapeDtypeStruct((rows, cols)...]
    unnamed x12 -> x0, local copies, waits for them, and re-layouts: 6.54 us -> none
    reshape x2 -> x0, local copies, waits for them, and re-layouts: 1.53 us -> none  [the longest x1 0.76 us: on_device(): section_cells.reshape(-1, chunk)]
    pallas_call x1, Pallas kernels: 17 us -> 18 us  [on_device(): pl.pallas_call(exchange_kernel, out_shape=(jax.ShapeDtypeStruct((5, SLABS...]
where the time goes in v2:
time: 29.5 us; the launch traced here: 29.3 us
  Pallas kernels  28.7 us (97%)
  between operations  0.64 us (2%)
    pallas_call x1, Pallas kernels, on_device(): pl.pallas_call(exchange_kernel, out_shape=(jax.ShapeDtypeStruct((5, SLABS...  18 us
    pallas_call x1, Pallas kernels, on_device(): pl.pallas_call(chain_kernel, out_shape=(jax.ShapeDtypeStruct((rows, cols)...  10.7 us

profile of v2, /device:TPU:1, one launch (start us, length us, event | category | flops | bytes accessed | tf_op | source)
XLA Modules:
  0.0 29.3 jit_solution(1455405850961352210)
XLA Ops:
  0.6 18.0 %exchange.1 = (f32[5,7,144,128]{3,2,1,0:T(8,128)}, f32[7,144,128]{2,1,0:T(8,128)}) custom-call(f32[3,768,128]{2,1,0:T(8,128)} %init_hbm.1, f32[768,128]{1,0:T(8,128)} %drag_hbm.1, f32[768,128]{1,0:T(8,128)} %dir_hbm.1, s32[768,128]{1,0:T(8,128)} %mask_hbm.1, s32[64,128]{1,0:T(8,128)} %bitcast.2, s32[64,128]{1,0:T(8,128)} %bitcast.3), custom_call_target="tpu_custom_call" | custom-call | tf_op jit(solution)/shard_map/exchange/pallas_call | solution.py:417
  18.6 10.7 %chain.1 = (f32[768,128]{1,0:T(8,128)}, f32[3,768,128]{2,1,0:T(8,128)}, f32[3,768,128]{2,1,0:T(8,128)}) custom-call(f32[5,7,144,128]{3,2,1,0:T(8,128)} %get-tuple-element.5.t_hbm, f32[7,144,128]{2,1,0:T(8,128)} %get-tuple-element.6.w_hbm), custom_call_target="tpu_custom_call" | custom-call | tf_op jit(solution)/shard_map/chain/pallas_call | solution.py:452

commit v3 on v2

--- a/solution.py
+++ b/solution.py
@@ -11,22 +11,32 @@
 SLABS = 7
 LOW = (SLABS + 1) // 2
 PAD = 8
+HALO_LANES = (17, 24, 49, 56, 81)
 CHUNK = 8
 MESH = pl.DeviceIdType.MESH
 
 
+def patched(tile, halo_rows, f, j):
+    lane = lax.broadcasted_iota(jnp.int32, tile.shape, 1)
+    rolled = pltpu.roll(halo_rows, (128 - HALO_LANES[f] - j) % 128, 1)
+    north = 111 if j < 4 else 110
+    here = lane == 0 if j == 4 else (lane == 0) | (lane == north)
+    return jnp.where(here, rolled, tile)
+
+
 def exchange_kernel(
     init_hbm, drag_hbm, dir_hbm, mask_hbm, cells_hbm, sign_hbm,
-    t_hbm, w_hbm,
+    t_hbm, patch_hbm, w_hbm,
     t_ref, w_ref, init_ref, drag_ref, dir_ref, mask_ref, cells_ref, sign_ref,
-    nat, flip, at_ref, acc, fold_acc, load_sem, send_sem, recv_sem, out_sem,
+    nat, edge, strip, from_west, from_east, north_tile, halo, pack, patch, side,
+    at_ref, acc, fold_acc, load_sem, send_sem, recv_sem, out_sem,
 ):
     rows, cols = drag_ref.shape
     ext = cols + 2 * PAD
     n_lon, n_lat = lax.axis_size("lon"), lax.axis_size("lat")
     lon, lat = lax.axis_index("lon"), lax.axis_index("lat")
     top = lat == n_lat - 1
-    east, west = lax.rem(lon + 1, n_lon), lax.rem(lon + n_lon - 1, n_lon)
+    inner = lat > 0
 
     loads = [
         pltpu.make_async_copy(src, dst, load_sem.at[k])
@@ -38,114 +48,155 @@
     for load in loads:
         load.start()
 
+    def around(at, by):
+        return lax.rem(at + by + n_lon, n_lon)
+
+    up_lat = jnp.where(top, lat, lat + 1)
+    up_lon = jnp.where(top, n_lon - 1 - lon, lon)
+    up_slot = jnp.where(top, 3, 0)
+    turns = (0, 1, -1)
+    ups = [around(up_lon, by) for by in turns]
+    downs = [around(lon, by) for by in turns]
+    own_fold = [top & (at == lon) for at in ups]
+
     def device(lon_at, lat_at):
         return {"lon": lon_at, "lat": lat_at}
 
     barrier = pltpu.get_barrier_semaphore()
 
-    def greet(target):
-        pl.semaphore_signal(barrier, inc=1, device_id=target, device_id_type=MESH)
-
-    greet(device(east, lat))
-    greet(device(west, lat))
-
-    @pl.when(top)
-    def _():
-        greet(device(n_lon - 1 - lon, lat))
-
-    @pl.when(jnp.logical_not(top))
-    def _():
-        greet(device(lon, lat + 1))
-
-    @pl.when(lat > 0)
-    def _():
-        greet(device(lon, lat - 1))
+    def greet(lon_at, lat_at):
+        pl.semaphore_signal(
+            barrier, inc=1, device_id=device(lon_at, lat_at), device_id_type=MESH
+        )
+
+    greet(around(lon, 1), lat)
+    greet(around(lon, -1), lat)
+    peers = 2
+    for k in range(3):
+        pl.when(jnp.logical_not(own_fold[k]))(functools.partial(greet, ups[k], up_lat))
+        pl.when(inner)(functools.partial(greet, downs[k], lat - 1))
+        peers += jnp.where(own_fold[k], 0, 1) + jnp.where(inner, 1, 0)
+
+    lane_of = lax.broadcasted_iota(jnp.int32, (64, cols), 1)
 
     def prepare(part, carry):
         here = pl.ds(pl.multiple_of(part * 64, 64), 64)
         there = pl.ds(pl.multiple_of(part * 64 + PAD, 8), 64)
         ocean = mask_ref[here, :].astype(jnp.float32)
         inverse = 1.0 / (1.0 + drag_ref[here, :])
-        nat[0, there, :] = init_ref[0, here, :] * (0.2 * ocean)
-        nat[1, there, :] = init_ref[1, here, :] * ocean
-        nat[2, there, :] = init_ref[2, here, :] * ocean
-        nat[3, there, :] = ocean * inverse
-        nat[4, there, :] = -(dir_ref[here, :] * inverse)
+        fields = [
+            init_ref[0, here, :] * (0.2 * ocean),
+            init_ref[1, here, :] * ocean,
+            init_ref[2, here, :] * ocean,
+            ocean * inverse,
+            -(dir_ref[here, :] * inverse),
+        ]
+        sides = pltpu.roll(fields[0], 8, 1)
+        for f in range(5):
+            nat[f, there, :] = fields[f]
+            if f:
+                sides = jnp.where(
+                    lane_of < 16 * f, sides, pltpu.roll(fields[f], 16 * f + 8, 1)
+                )
+        edge[there, :] = sides
         return carry
 
-    tail = rows + 2 * PAD
+    height = nat.shape[1]
+    tail = rows + PAD
     for f in range(5):
-        nat[f, tail:, :] = jnp.zeros((nat.shape[1] - tail, cols), jnp.float32)
+        nat[f, 0:PAD, :] = jnp.zeros((PAD, cols), jnp.float32)
+        nat[f, tail:, :] = jnp.zeros((height - tail, cols), jnp.float32)
+    edge[0:PAD, :] = jnp.zeros((PAD, cols), jnp.float32)
+    edge[tail:, :] = jnp.zeros((height - tail, cols), jnp.float32)
     for load in loads:
         load.wait()
     lax.fori_loop(0, rows // 64, prepare, 0)
 
-    lanes = lax.broadcasted_iota(jnp.int32, (PAD, cols), 1)
-    for f in range(5):
-        tile = nat[f, rows : rows + PAD, :]
-        turned = jnp.take_along_axis(tile, cols - 1 - lanes, axis=1)
-        if f in (1, 2):
-            turned = -turned
-        for k in range(PAD):
-            flip[f, k : k + 1, :] = turned[PAD - 1 - k : PAD - k, :]
-
-    south_halo, north_halo = pl.ds(0, PAD), pl.ds(rows + PAD, PAD)
-
-    def copy(src, dst, which, slot, target):
+    @pl.when(jnp.logical_not(top))
+    def _():
+        north_tile[...] = nat[:, rows : rows + PAD, :]
+
+    @pl.when(top)
+    def _():
+        lanes = lax.broadcasted_iota(jnp.int32, (PAD, cols), 1)
+        for f in range(5):
+            tile = nat[f, rows : rows + PAD, :]
+            turned = jnp.take_along_axis(tile, cols - 1 - lanes, axis=1)
+            if f in (1, 2):
+                turned = -turned
+            for k in range(PAD):
+                north_tile[f, k : k + 1, :] = turned[PAD - 1 - k : PAD - k, :]
+
+    @pl.when(lat == 0)
+    def _():
+        for k in range(3):
+            halo[k] = jnp.zeros((5, PAD, cols), jnp.float32)
+
+    for k in range(1, 3):
+        @pl.when(own_fold[k])
+        def _():
+            halo[3 + k] = north_tile[...]
+
+    def copy(src, dst, which, slot, lon_at, lat_at):
         return pltpu.make_async_remote_copy(
             src_ref=src, dst_ref=dst, send_sem=send_sem.at[which],
-            recv_sem=recv_sem.at[slot], device_id=target, device_id_type=MESH,
-        )
-
-    fold_copy = copy(flip, nat.at[:, north_halo, :], 0, 1, device(n_lon - 1 - lon, lat))
-    north_copy = copy(
-        nat.at[:, pl.ds(rows, PAD), :], nat.at[:, south_halo, :], 0, 0, device(lon, lat + 1)
-    )
-    south_copy = copy(
-        nat.at[:, pl.ds(PAD, PAD), :], nat.at[:, north_halo, :], 1, 1, device(lon, lat - 1)
-    )
+            recv_sem=recv_sem.at[slot], device_id=device(lon_at, lat_at),
+            device_id_type=MESH,
+        )
+
+    up_copies = [
+        copy(north_tile, halo.at[up_slot + k], k, up_slot + k, ups[k], up_lat)
+        for k in range(3)
+    ]
+    down_copies = [
+        copy(nat.at[:, pl.ds(PAD, PAD), :], halo.at[3 + k], 3 + k, 3 + k, downs[k], lat - 1)
+        for k in range(3)
+    ]
     east_copy = copy(
-        t_ref.at[:, :, pl.ds(cols, PAD), :], t_ref.at[:, :, pl.ds(0, PAD), :],
-        2, 2, device(east, lat),
+        strip.at[:, pl.ds(0, 5), pl.ds(0, 8), :], from_west, 6, 6, around(lon, 1), lat
     )
     west_copy = copy(
-        t_ref.at[:, :, pl.ds(PAD, PAD), :], t_ref.at[:, :, pl.ds(cols + PAD, PAD), :],
-        3, 3, device(west, lat),
+        strip.at[:, pl.ds(0, 5), pl.ds(8, 8), :], from_east, 7, 7, around(lon, -1), lat
     )
 
-    pl.semaphore_wait(barrier, jnp.where(lat > 0, 4, 3))
-
-    @pl.when(top)
-    def _():
-        fold_copy.start()
-
-    @pl.when(jnp.logical_not(top))
-    def _():
-        north_copy.start()
-
-    @pl.when(lat > 0)
-    def _():
-        south_copy.start()
-
-    @pl.when(lat == 0)
-    def _():
+    pl.semaphore_wait(barrier, peers)
+    for k in range(3):
+        pl.when(jnp.logical_not(own_fold[k]))(up_copies[k].start)
+        pl.when(inner)(down_copies[k].start)
+    for j in range(SLABS):
+        turned = edge[pl.ds(j + 1, 128, stride=SLABS), :].T
         for f in range(5):
-            nat[f, 0:PAD, :] = jnp.zeros((PAD, cols), jnp.float32)
+            strip[j, f] = turned[16 * f : 16 * f + 16]
+    east_copy.start()
+    west_copy.start()
+
+    for f in range(5):
+        for j in range(SLABS):
+            t_ref[f, j, PAD : cols + PAD, :] = nat[f, pl.ds(j + 1, 128, stride=SLABS), :].T
+
+    def store(start, size, which):
+        part = pl.ds(start, size)
+        return pltpu.make_async_copy(
+            t_ref.at[:, :, part, :], t_hbm.at[:, :, part, :], out_sem.at[which]
+        )
+
+    own_out = store(PAD, cols, 0)
+    own_out.start()
 
     total = cols * n_lon
     cell = cells_ref[...]
     row, col = lax.div(cell, total), lax.rem(cell, total)
-    r = row - lat * rows + PAD
+    r = row - lat * rows + SLABS
     lane = lax.shift_right_arithmetic(r * 9363, 16)
     slab = r - lane * SLABS
     c = col - lon * cols + PAD
     c = jnp.where(c < 0, c + total, c)
     c = jnp.where(c >= total, c - total, c)
-    in_rows = (r >= 0) & (r < rows + 2 * PAD)
+    in_rows = (r >= 0) & (r < rows + 2 * SLABS)
     at_ref[0] = jnp.where(c < ext, lax.div(slab, LOW) * ext + c, -1)
     at_ref[1] = jnp.where(in_rows, lax.rem(slab, LOW) * 128 + lane, -1)
     fr = rows - 1 - (row - lat * rows)
-    at_ref[2] = jnp.where(top & (fr < PAD), fr, -1)
+    at_ref[2] = jnp.where(top & (fr < SLABS), fr, -1)
     fc = total - 1 - col - lon * cols + PAD
     fc = jnp.where(fc < 0, fc + total, fc)
     at_ref[3] = jnp.where(fc >= total, fc - total, fc)
@@ -187,38 +238,14 @@
         )
         return carry
 
-    parts = cells_ref.shape[0] // CHUNK
-    lax.fori_loop(0, parts // 2, gather_weights, 0)
-
-    @pl.when(lat > 0)
-    def _():
-        north_copy.wait_recv()
-
-    south_copy.wait_recv()
-
-    for f in range(5):
-        for j in range(SLABS):
-            t_ref[f, j, PAD : cols + PAD, :] = nat[f, pl.ds(j, 128, stride=SLABS), :].T
-    east_copy.start()
-    west_copy.start()
-
-    def store(start, size, which):
-        part = pl.ds(start, size)
-        return pltpu.make_async_copy(
-            t_ref.at[:, :, part, :], t_hbm.at[:, :, part, :], out_sem.at[which]
-        )
-
-    own_out = store(PAD, cols, 0)
-    own_out.start()
-
-    lax.fori_loop(parts // 2, parts, gather_weights, 0)
+    lax.fori_loop(0, cells_ref.shape[0] // CHUNK, gather_weights, 0)
     column = lax.broadcasted_iota(jnp.int32, (ext, 128), 1)
     ghosts = fold_acc[...]
     for j in range(SLABS):
         hi, lo = divmod(j, LOW)
         found = acc[hi * ext : (hi + 1) * ext, lo * 128 : (lo + 1) * 128]
-        for k in range(PAD):
-            lane_at, slab_at = divmod(rows + PAD + k, SLABS)
+        for k in range(SLABS):
+            lane_at, slab_at = divmod(rows + SLABS + k, SLABS)
             if slab_at == j:
                 turned = pltpu.roll(ghosts, lane_at - k, 1)
                 found -= jnp.where(column == lane_at, turned, 0.0)
@@ -226,29 +253,50 @@
     w_out = pltpu.make_async_copy(w_ref, w_hbm, out_sem.at[1])
     w_out.start()
 
-    east_copy.wait_recv()
-    east_out = store(0, PAD, 2)
+    for k in range(3):
+        pl.when(inner)(
+            copy(north_tile, halo.at[k], k, k, ups[k], up_lat).wait_recv
+        )
+        pl.when(jnp.logical_not(own_fold[k]))(
+            copy(north_tile, halo.at[3 + k], k, 3 + k, ups[k], up_lat).wait_recv
+        )
+    pack[...] = jnp.zeros_like(pack)
+    for k in range(3):
+        for f in range(5):
+            at = HALO_LANES[f]
+            pack[k, at : at + 7, :] = halo[k, f, 1:8, :]
+            pack[k, at - 17 : at - 13, :] = halo[3 + k, f, 2:6, :]
+            pack[k, at - 13 : at - 11, :] = halo[3 + k, f, 0:2, :]
+    patch[...] = pack[0].T
+    patch_out = pltpu.make_async_copy(patch, patch_hbm, out_sem.at[2])
+    patch_out.start()
+    side[0] = pack[1].T[cols - PAD : cols]
+    side[1] = pack[2].T[0:PAD]
+    for k, got, sent, place in ((0, from_west, east_copy, 0), (1, from_east, west_copy, cols + PAD)):
+        sent.wait_recv()
+        for f in range(5):
+            for j in range(SLABS):
+                t_ref[f, j, place : place + PAD, :] = patched(got[j, f], side[k], f, j)
+    west_out = store(0, PAD, 3)
+    west_out.start()
+    east_out = store(cols + PAD, PAD, 4)
     east_out.start()
-    west_copy.wait_recv()
-    west_out = store(cols + PAD, PAD, 3)
-    west_out.start()
+
     east_copy.wait_send()
     west_copy.wait_send()
-    north_copy.wait_send()
-
-    @pl.when(lat > 0)
-    def _():
-        south_copy.wait_send()
-
+    for k in range(3):
+        pl.when(jnp.logical_not(own_fold[k]))(up_copies[k].wait_send)
+        pl.when(inner)(down_copies[k].wait_send)
     own_out.wait()
     w_out.wait()
+    patch_out.wait()
+    west_out.wait()
     east_out.wait()
-    west_out.wait()
 
 
 def chain_kernel(
-    t_hbm, w_hbm, curv_hbm, state_hbm, tangent_hbm,
-    t_ref, w_ref, levels, back_a, back_b, scale_ref, curv, nat, load_sem, out_sem,
+    t_hbm, patch_hbm, w_hbm, curv_hbm, state_hbm, tangent_hbm,
+    t_ref, patch_ref, w_ref, levels, back_a, back_b, scale_ref, curv, nat, load_sem, out_sem,
 ):
     ext = t_ref.shape[2]
     cols = ext - 2 * PAD
@@ -256,6 +304,8 @@
     tiles = ext // 8
     third = ext // 3
 
+    patch_load = pltpu.make_async_copy(patch_hbm, patch_ref, load_sem.at[4])
+    patch_load.start()
     loads = [
         pltpu.make_async_copy(
             t_hbm.at[:, :, pl.ds(k * third, third), :],
@@ -335,18 +385,26 @@
             block = levels[ITERS - 1, field, j, PAD : PAD + cols, :]
             if times is not None:
                 block = block * times
-            nat[field, pl.ds(j, 128, stride=SLABS), :] = block.T
+            nat[field, pl.ds(j + 1, 128, stride=SLABS), :] = block.T
 
     def send(field, out, at):
         return pltpu.make_async_copy(
             nat.at[field, pl.ds(PAD, rows), :], out.at[at], out_sem.at[field]
         )
 
-    ready = 0
-    for i in range(tiles):
-        while ready < 3 and ready * third < 8 * i + 9:
-            loads[ready].wait()
-            ready += 1
+    patch_load.wait()
+    for i in range(tiles + 1):
+        if i % (tiles // 3) == 0 and i < tiles:
+            loads[i // (tiles // 3)].wait()
+        if 0 < i < tiles - 1:
+            here = slice(8 * i, 8 * i + 8)
+            halo_rows = patch_ref[8 * i - PAD : 8 * i - PAD + 8, :]
+            for f in range(5):
+                for j in range(SLABS):
+                    t_ref[f, j, here, :] = patched(t_ref[f, j, here, :], halo_rows, f, j)
+        if i == 0:
+            continue
+        i -= 1
         step(t_ref, levels.at[0], i, 0.25, first=True)
 
     def forward(n, carry):
@@ -399,7 +457,7 @@
 
     lax.fori_loop(0, (ITERS - 2) // 2, backward, 0)
     for j in range(SLABS):
-        nat[6, pl.ds(j, 128, stride=SLABS), :] = curv[j].T
+        nat[6, pl.ds(j + 1, 128, stride=SLABS), :] = curv[j].T
     curv_copy = pltpu.make_async_copy(nat.at[6, pl.ds(PAD, rows), :], curv_hbm, out_sem.at[6])
     curv_copy.start()
     for f in range(3):
@@ -414,32 +472,42 @@
     f32, i32 = jnp.float32, jnp.int32
     hbm = pl.BlockSpec(memory_space=pl.ANY)
     lines = section_cells.shape[0] // 128
-    fields, weights = pl.pallas_call(
+    tall = SLABS * 128 + 8
+    vm, dma = pltpu.VMEM, pltpu.SemaphoreType.DMA
+    fields = jax.ShapeDtypeStruct((5, SLABS, ext, 128), f32)
+    weights = jax.ShapeDtypeStruct((SLABS, ext, 128), f32)
+    patches = jax.ShapeDtypeStruct((cols, 128), f32)
+    fields, patches, weights = pl.pallas_call(
         exchange_kernel,
-        out_shape=(
-            jax.ShapeDtypeStruct((5, SLABS, ext, 128), f32),
-            jax.ShapeDtypeStruct((SLABS, ext, 128), f32),
-        ),
+        out_shape=(fields, patches, weights),
         in_specs=[hbm] * 6,
-        out_specs=(hbm, hbm),
+        out_specs=(hbm, hbm, hbm),
         scratch_shapes=[
-            pltpu.VMEM((5, SLABS, ext, 128), f32),
-            pltpu.VMEM((SLABS, ext, 128), f32),
-            pltpu.VMEM((3, rows, cols), f32),
-            pltpu.VMEM((rows, cols), f32),
-            pltpu.VMEM((rows, cols), f32),
-            pltpu.VMEM((rows, cols), i32),
-            pltpu.VMEM((lines, 128), i32),
-            pltpu.VMEM((lines, 128), i32),
-            pltpu.VMEM((5, SLABS * 128, cols), f32),
-            pltpu.VMEM((5, PAD, cols), f32),
-            pltpu.VMEM((4, lines, 128), i32),
-            pltpu.VMEM((2 * ext, LOW * 128), f32),
-            pltpu.VMEM((ext, 128), f32),
-            pltpu.SemaphoreType.DMA((6,)),
-            pltpu.SemaphoreType.DMA((4,)),
-            pltpu.SemaphoreType.DMA((4,)),
-            pltpu.SemaphoreType.DMA((4,)),
+            vm(fields.shape, f32),
+            vm(weights.shape, f32),
+            vm((3, rows, cols), f32),
+            vm((rows, cols), f32),
+            vm((rows, cols), f32),
+            vm((rows, cols), i32),
+            vm((lines, 128), i32),
+            vm((lines, 128), i32),
+            vm((5, tall, cols), f32),
+            vm((tall, cols), f32),
+            vm((SLABS, 5, 16, 128), f32),
+            vm((SLABS, 5, 8, 128), f32),
+            vm((SLABS, 5, 8, 128), f32),
+            vm((5, PAD, cols), f32),
+            vm((6, 5, PAD, cols), f32),
+            vm((3, 128, cols), f32),
+            vm((cols, 128), f32),
+            vm((2, 8, 128), f32),
+            vm((4, lines, 128), i32),
+            vm((2 * ext, LOW * 128), f32),
+            vm((ext, 128), f32),
+            dma((6,)),
+            dma((8,)),
+            dma((8,)),
+            dma((5,)),
         ],
         compiler_params=pltpu.CompilerParams(
             collective_id=0, has_side_effects=True, vmem_limit_bytes=56 * 1024 * 1024
@@ -456,23 +524,24 @@
             jax.ShapeDtypeStruct((3, rows, cols), f32),
             jax.ShapeDtypeStruct((3, rows, cols), f32),
         ),
-        in_specs=[hbm] * 2,
+        in_specs=[hbm] * 3,
         out_specs=(hbm, hbm, hbm),
         scratch_shapes=[
-            pltpu.VMEM((5, SLABS, ext, 128), f32),
-            pltpu.VMEM((SLABS, ext, 128), f32),
-            pltpu.VMEM((ITERS, 6, SLABS, ext, 128), f32),
-            pltpu.VMEM((6, SLABS, ext, 128), f32),
-            pltpu.VMEM((6, SLABS, ext, 128), f32),
-            pltpu.VMEM((SLABS, ext, 128), f32),
-            pltpu.VMEM((SLABS, cols, 128), f32),
-            pltpu.VMEM((7, SLABS * 128, cols), f32),
-            pltpu.SemaphoreType.DMA((4,)),
-            pltpu.SemaphoreType.DMA((7,)),
+            vm(fields.shape, f32),
+            vm(patches.shape, f32),
+            vm(weights.shape, f32),
+            vm((ITERS, 6, SLABS, ext, 128), f32),
+            vm((6, SLABS, ext, 128), f32),
+            vm((6, SLABS, ext, 128), f32),
+            vm((SLABS, ext, 128), f32),
+            vm((SLABS, cols, 128), f32),
+            vm((7, tall, cols), f32),
+            dma((5,)),
+            dma((7,)),
         ],
         compiler_params=pltpu.CompilerParams(vmem_limit_bytes=56 * 1024 * 1024),
         name="chain",
-    )(fields, weights)
+    )(fields, patches, weights)
 
 
 def solution(mesh):

time: 29.5 us -> 29 us (0.983)
  Pallas kernels: 28.7 us -> 28.2 us
    pallas_call x1, Pallas kernels: 18 us -> 17 us  [on_device(): pl.pallas_call(exchange_kernel, out_shape=(fields, patches, weights), in_...]
    pallas_call x1, Pallas kernels: 10.7 us -> 11.2 us  [on_device(): pl.pallas_call(chain_kernel, out_shape=(jax.ShapeDtypeStruct((rows, cols)...]
where the time goes in v3:
time: 29 us; the launch traced here: 28.8 us
  Pallas kernels  28.2 us (97%)
  between operations  0.64 us (2%)
    pallas_call x1, Pallas kernels, on_device(): pl.pallas_call(exchange_kernel, out_shape=(fields, patches, weights), in_...  17 us
    pallas_call x1, Pallas kernels, on_device(): pl.pallas_call(chain_kernel, out_shape=(jax.ShapeDtypeStruct((rows, cols)...  11.2 us

profile of v3, /device:TPU:1, one launch (start us, length us, event | category | flops | bytes accessed | tf_op | source)
XLA Modules:
  0.0 28.8 jit_solution(12169853196600326026)
XLA Ops:
  0.6 17.0 %exchange.1 = (f32[5,7,144,128]{3,2,1,0:T(8,128)}, f32[128,128]{1,0:T(8,128)}, f32[7,144,128]{2,1,0:T(8,128)}) custom-call(f32[3,768,128]{2,1,0:T(8,128)} %init_hbm.1, f32[768,128]{1,0:T(8,128)} %drag_hbm.1, f32[768,128]{1,0:T(8,128)} %dir_hbm.1, s32[768,128]{1,0:T(8,128)} %mask_hbm.1, s32[64,128]{1,0:T(8,128)} %bitcast.2, s32[64,128]{1,0:T(8,128)} %bitcast.3), custom_call_target="tpu_custom_call" | custom-call | tf_op jit(solution)/shard_map/exchange/pallas_call | solution.py:480
  17.6 11.2 %chain.1 = (f32[768,128]{1,0:T(8,128)}, f32[3,768,128]{2,1,0:T(8,128)}, f32[3,768,128]{2,1,0:T(8,128)}) custom-call(f32[5,7,144,128]{3,2,1,0:T(8,128)} %get-tuple-element.6.t_hbm, f32[128,128]{1,0:T(8,128)} %get-tuple-element.7.patch_hbm, f32[7,144,128]{2,1,0:T(8,128)} %get-tuple-element.8.w_hbm), custom_call_target="tpu_custom_call" | custom-call | tf_op jit(solution)/shard_map/chain/pallas_call | solution.py:520

commit v4 on v3

--- a/solution.py
+++ b/solution.py
@@ -26,10 +26,9 @@
 
 def exchange_kernel(
     init_hbm, drag_hbm, dir_hbm, mask_hbm, cells_hbm, sign_hbm,
-    t_hbm, patch_hbm, w_hbm,
+    t_hbm, halo, from_west, from_east, w_hbm,
     t_ref, w_ref, init_ref, drag_ref, dir_ref, mask_ref, cells_ref, sign_ref,
-    nat, edge, strip, from_west, from_east, north_tile, halo, pack, patch, side,
-    at_ref, acc, fold_acc, load_sem, send_sem, recv_sem, out_sem,
+    nat, edge, strip, north_tile, at_ref, acc, fold_acc, load_sem, send_sem, recv_sem, out_sem,
 ):
     rows, cols = drag_ref.shape
     ext = cols + 2 * PAD
@@ -45,9 +44,6 @@
             (dir_hbm, dir_ref), (cells_hbm, cells_ref), (sign_hbm, sign_ref),
         ))
     ]
-    for load in loads:
-        load.start()
-
     def around(at, by):
         return lax.rem(at + by + n_lon, n_lon)
 
@@ -76,6 +72,8 @@
         pl.when(jnp.logical_not(own_fold[k]))(functools.partial(greet, ups[k], up_lat))
         pl.when(inner)(functools.partial(greet, downs[k], lat - 1))
         peers += jnp.where(own_fold[k], 0, 1) + jnp.where(inner, 1, 0)
+    for load in loads:
+        load.start()
 
     lane_of = lax.broadcasted_iota(jnp.int32, (64, cols), 1)
 
@@ -108,7 +106,7 @@
         nat[f, tail:, :] = jnp.zeros((height - tail, cols), jnp.float32)
     edge[0:PAD, :] = jnp.zeros((PAD, cols), jnp.float32)
     edge[tail:, :] = jnp.zeros((height - tail, cols), jnp.float32)
-    for load in loads:
+    for load in loads[:4]:
         load.wait()
     lax.fori_loop(0, rows // 64, prepare, 0)
 
@@ -127,15 +125,19 @@
             for k in range(PAD):
                 north_tile[f, k : k + 1, :] = turned[PAD - 1 - k : PAD - k, :]
 
-    @pl.when(lat == 0)
-    def _():
-        for k in range(3):
-            halo[k] = jnp.zeros((5, PAD, cols), jnp.float32)
-
-    for k in range(1, 3):
-        @pl.when(own_fold[k])
-        def _():
-            halo[3 + k] = north_tile[...]
+    def fill(src, slot):
+        return pltpu.make_async_copy(src, halo.at[slot], out_sem.at[2 + slot])
+
+    zeros = nat.at[:, pl.ds(tail, PAD), :]
+    lowest = jnp.logical_not(inner)
+    for k in range(3):
+        pl.when(lowest)(fill(zeros, k).start)
+        pl.when(own_fold[k])(fill(north_tile, 3 + k).start)
+
+    for j in range(SLABS):
+        turned = edge[pl.ds(j + 1, 128, stride=SLABS), :].T
+        for f in range(5):
+            strip[j, f] = turned[16 * f : 16 * f + 16]
 
     def copy(src, dst, which, slot, lon_at, lat_at):
         return pltpu.make_async_remote_copy(
@@ -160,28 +162,19 @@
     )
 
     pl.semaphore_wait(barrier, peers)
-    for k in range(3):
+    east_copy.start()
+    west_copy.start()
+    for k in (1, 2, 0):
         pl.when(jnp.logical_not(own_fold[k]))(up_copies[k].start)
         pl.when(inner)(down_copies[k].start)
-    for j in range(SLABS):
-        turned = edge[pl.ds(j + 1, 128, stride=SLABS), :].T
-        for f in range(5):
-            strip[j, f] = turned[16 * f : 16 * f + 16]
-    east_copy.start()
-    west_copy.start()
 
     for f in range(5):
         for j in range(SLABS):
-            t_ref[f, j, PAD : cols + PAD, :] = nat[f, pl.ds(j + 1, 128, stride=SLABS), :].T
-
-    def store(start, size, which):
-        part = pl.ds(start, size)
-        return pltpu.make_async_copy(
-            t_ref.at[:, :, part, :], t_hbm.at[:, :, part, :], out_sem.at[which]
-        )
-
-    own_out = store(PAD, cols, 0)
+            t_ref[f, j] = nat[f, pl.ds(j + 1, 128, stride=SLABS), :].T
+    own_out = pltpu.make_async_copy(t_ref, t_hbm, out_sem.at[0])
     own_out.start()
+    for load in loads[4:]:
+        load.wait()
 
     total = cols * n_lon
     cell = cells_ref[...]
@@ -260,60 +253,42 @@
         pl.when(jnp.logical_not(own_fold[k]))(
             copy(north_tile, halo.at[3 + k], k, 3 + k, ups[k], up_lat).wait_recv
         )
-    pack[...] = jnp.zeros_like(pack)
-    for k in range(3):
-        for f in range(5):
-            at = HALO_LANES[f]
-            pack[k, at : at + 7, :] = halo[k, f, 1:8, :]
-            pack[k, at - 17 : at - 13, :] = halo[3 + k, f, 2:6, :]
-            pack[k, at - 13 : at - 11, :] = halo[3 + k, f, 0:2, :]
-    patch[...] = pack[0].T
-    patch_out = pltpu.make_async_copy(patch, patch_hbm, out_sem.at[2])
-    patch_out.start()
-    side[0] = pack[1].T[cols - PAD : cols]
-    side[1] = pack[2].T[0:PAD]
-    for k, got, sent, place in ((0, from_west, east_copy, 0), (1, from_east, west_copy, cols + PAD)):
-        sent.wait_recv()
-        for f in range(5):
-            for j in range(SLABS):
-                t_ref[f, j, place : place + PAD, :] = patched(got[j, f], side[k], f, j)
-    west_out = store(0, PAD, 3)
-    west_out.start()
-    east_out = store(cols + PAD, PAD, 4)
-    east_out.start()
-
+        pl.when(lowest)(fill(zeros, k).wait)
+        pl.when(own_fold[k])(fill(north_tile, 3 + k).wait)
+        pl.when(jnp.logical_not(own_fold[k]))(up_copies[k].wait_send)
+        pl.when(inner)(down_copies[k].wait_send)
     east_copy.wait_send()
     west_copy.wait_send()
-    for k in range(3):
-        pl.when(jnp.logical_not(own_fold[k]))(up_copies[k].wait_send)
-        pl.when(inner)(down_copies[k].wait_send)
     own_out.wait()
     w_out.wait()
-    patch_out.wait()
-    west_out.wait()
-    east_out.wait()
+    east_copy.wait_recv()
+    west_copy.wait_recv()
 
 
 def chain_kernel(
-    t_hbm, patch_hbm, w_hbm, curv_hbm, state_hbm, tangent_hbm,
-    t_ref, patch_ref, w_ref, levels, back_a, back_b, scale_ref, curv, nat, load_sem, out_sem,
+    t_hbm, halo_hbm, west_hbm, east_hbm, w_hbm, curv_hbm, state_hbm, tangent_hbm,
+    t_ref, halo, from_west, from_east, pack, patch, w_ref, levels, back_a, back_b, scale_ref, curv, nat, load_sem, out_sem,
 ):
     ext = t_ref.shape[2]
     cols = ext - 2 * PAD
     rows = curv_hbm.shape[0]
     tiles = ext // 8
-    third = ext // 3
-
-    patch_load = pltpu.make_async_copy(patch_hbm, patch_ref, load_sem.at[4])
-    patch_load.start()
+    bounds = (0, 16, 64, cols)
+    sides = [
+        pltpu.make_async_copy(src, dst, load_sem.at[k])
+        for k, (src, dst) in enumerate((
+            (halo_hbm, halo), (west_hbm, from_west), (east_hbm, from_east)
+        ))
+    ]
     loads = [
         pltpu.make_async_copy(
-            t_hbm.at[:, :, pl.ds(k * third, third), :],
-            t_ref.at[:, :, pl.ds(k * third, third), :], load_sem.at[k],
-        )
-        for k in range(3)
-    ] + [pltpu.make_async_copy(w_hbm, w_ref, load_sem.at[3])]
-    for load in loads:
+            t_hbm.at[:, :, pl.ds(low, high - low), :],
+            t_ref.at[:, :, pl.ds(PAD + low, high - low), :], load_sem.at[3 + k],
+        )
+        for k, (low, high) in enumerate(zip(bounds, bounds[1:]))
+    ]
+    w_load = pltpu.make_async_copy(w_hbm, w_ref, load_sem.at[6])
+    for load in sides + loads + [w_load]:
         load.start()
 
     def around(src, field, j, i):
@@ -392,19 +367,33 @@
             nat.at[field, pl.ds(PAD, rows), :], out.at[at], out_sem.at[field]
         )
 
-    patch_load.wait()
-    for i in range(tiles + 1):
-        if i % (tiles // 3) == 0 and i < tiles:
-            loads[i // (tiles // 3)].wait()
-        if 0 < i < tiles - 1:
-            here = slice(8 * i, 8 * i + 8)
-            halo_rows = patch_ref[8 * i - PAD : 8 * i - PAD + 8, :]
+    pack[...] = jnp.zeros_like(pack)
+    sides[0].wait()
+    for k in range(3):
+        for f in range(5):
+            at = HALO_LANES[f]
+            pack[k, at : at + 7, :] = halo[k, f, 1:8, :]
+            pack[k, at - 17 : at - 13, :] = halo[3 + k, f, 2:6, :]
+            pack[k, at - 13 : at - 11, :] = halo[3 + k, f, 0:2, :]
+    patch[...] = pack[0].T
+    corners = pack[1].T[cols - PAD : cols], pack[2].T[0:PAD]
+    sides[1].wait()
+    sides[2].wait()
+    for got, corner, place in zip((from_west, from_east), corners, (0, cols + PAD)):
+        for f in range(5):
+            for j in range(SLABS):
+                t_ref[f, j, place : place + PAD, :] = patched(got[j, f], corner, f, j)
+
+    for i in range(tiles):
+        for load, low in zip(loads, bounds):
+            if 8 * i == low:
+                load.wait()
+        if i < tiles - 2:
+            here = slice(8 * i + PAD, 8 * i + PAD + 8)
+            halo_rows = patch[8 * i : 8 * i + 8, :]
             for f in range(5):
                 for j in range(SLABS):
                     t_ref[f, j, here, :] = patched(t_ref[f, j, here, :], halo_rows, f, j)
-        if i == 0:
-            continue
-        i -= 1
         step(t_ref, levels.at[0], i, 0.25, first=True)
 
     def forward(n, carry):
@@ -414,7 +403,7 @@
 
     lax.fori_loop(0, ITERS - 1, forward, 0)
 
-    loads[3].wait()
+    w_load.wait()
     last, prior = levels.at[ITERS - 1], levels.at[ITERS - 2]
     for i in range(tiles):
         here = slice(8 * i, 8 * i + 8)
@@ -474,14 +463,15 @@
     lines = section_cells.shape[0] // 128
     tall = SLABS * 128 + 8
     vm, dma = pltpu.VMEM, pltpu.SemaphoreType.DMA
-    fields = jax.ShapeDtypeStruct((5, SLABS, ext, 128), f32)
+    fields = jax.ShapeDtypeStruct((5, SLABS, cols, 128), f32)
+    halos = jax.ShapeDtypeStruct((6, 5, PAD, cols), f32)
+    beside = jax.ShapeDtypeStruct((SLABS, 5, PAD, 128), f32)
     weights = jax.ShapeDtypeStruct((SLABS, ext, 128), f32)
-    patches = jax.ShapeDtypeStruct((cols, 128), f32)
-    fields, patches, weights = pl.pallas_call(
+    given = pl.pallas_call(
         exchange_kernel,
-        out_shape=(fields, patches, weights),
+        out_shape=(fields, halos, beside, beside, weights),
         in_specs=[hbm] * 6,
-        out_specs=(hbm, hbm, hbm),
+        out_specs=(hbm,) * 5,
         scratch_shapes=[
             vm(fields.shape, f32),
             vm(weights.shape, f32),
@@ -494,20 +484,14 @@
             vm((5, tall, cols), f32),
             vm((tall, cols), f32),
             vm((SLABS, 5, 16, 128), f32),
-            vm((SLABS, 5, 8, 128), f32),
-            vm((SLABS, 5, 8, 128), f32),
             vm((5, PAD, cols), f32),
-            vm((6, 5, PAD, cols), f32),
-            vm((3, 128, cols), f32),
-            vm((cols, 128), f32),
-            vm((2, 8, 128), f32),
             vm((4, lines, 128), i32),
             vm((2 * ext, LOW * 128), f32),
             vm((ext, 128), f32),
             dma((6,)),
             dma((8,)),
             dma((8,)),
-            dma((5,)),
+            dma((8,)),
         ],
         compiler_params=pltpu.CompilerParams(
             collective_id=0, has_side_effects=True, vmem_limit_bytes=56 * 1024 * 1024
@@ -524,11 +508,15 @@
             jax.ShapeDtypeStruct((3, rows, cols), f32),
             jax.ShapeDtypeStruct((3, rows, cols), f32),
         ),
-        in_specs=[hbm] * 3,
+        in_specs=[hbm] * 5,
         out_specs=(hbm, hbm, hbm),
         scratch_shapes=[
-            vm(fields.shape, f32),
-            vm(patches.shape, f32),
+            vm((5, SLABS, ext, 128), f32),
+            vm(halos.shape, f32),
+            vm(beside.shape, f32),
+            vm(beside.shape, f32),
+            vm((3, 128, cols), f32),
+            vm((cols, 128), f32),
             vm(weights.shape, f32),
             vm((ITERS, 6, SLABS, ext, 128), f32),
             vm((6, SLABS, ext, 128), f32),
@@ -536,12 +524,12 @@
             vm((SLABS, ext, 128), f32),
             vm((SLABS, cols, 128), f32),
             vm((7, tall, cols), f32),
-            dma((5,)),
+            dma((7,)),
             dma((7,)),
         ],
         compiler_params=pltpu.CompilerParams(vmem_limit_bytes=56 * 1024 * 1024),
         name="chain",
-    )(fields, patches, weights)
+    )(*given)
 
 
 def solution(mesh):

time: 29 us -> 30.4 us (1.048)
  Pallas kernels: 28.2 us -> 29.6 us
    pallas_call x1, Pallas kernels: 17 us -> 18.3 us  [on_device(): pl.pallas_call(exchange_kernel, out_shape=(fields, halos, beside, beside,...]
where the time goes in v4:
time: 30.4 us; the launch traced here: 30.3 us
  Pallas kernels  29.6 us (97%)
  between operations  0.64 us (2%)
    pallas_call x1, Pallas kernels, on_device(): pl.pallas_call(exchange_kernel, out_shape=(fields, halos, beside, beside,...  18.3 us
    pallas_call x1, Pallas kernels, on_device(): pl.pallas_call(chain_kernel, out_shape=(jax.ShapeDtypeStruct((rows, cols)...  11.3 us

profile of v4, /device:TPU:1, one launch (start us, length us, event | category | flops | bytes accessed | tf_op | source)
XLA Modules:
  0.0 30.3 jit_solution(2755778362374200120)
XLA Ops:
  0.6 18.3 %exchange.1 = (f32[5,7,128,128]{3,2,1,0:T(8,128)}, f32[6,5,8,128]{3,2,1,0:T(8,128)}, f32[7,5,8,128]{3,2,1,0:T(8,128)}, f32[7,5,8,128]{3,2,1,0:T(8,128)}, f32[7,144,128]{2,1,0:T(8,128)}) custom-call(f32[3,768,128]{2,1,0:T(8,128)} %init_hbm.1, f32[768,128]{1,0:T(8,128)} %drag_hbm.1, f32[768,128]{1,0:T(8,128)} %dir_hbm.1, s32[768,128]{1,0:T(8,128)} %mask_hbm.1, ...), custom_call_target="tpu_custom_call" | custom-call | tf_op jit(solution)/shard_map/exchange/pallas_call | solution.py:470
  19.0 11.3 %chain.1 = (f32[768,128]{1,0:T(8,128)}, f32[3,768,128]{2,1,0:T(8,128)}, f32[3,768,128]{2,1,0:T(8,128)}) custom-call(f32[5,7,128,128]{3,2,1,0:T(8,128)} %get-tuple-element.8.t_hbm, f32[6,5,8,128]{3,2,1,0:T(8,128)} %get-tuple-element.9.halo_hbm, f32[7,5,8,128]{3,2,1,0:T(8,128)} %get-tuple-element.10.west_hbm, f32[7,5,8,128]{3,2,1,0:T(8,128)} %get-tuple-element.11.east_hbm, ...), custom_call_target="tpu_custom_call" | custom-call | tf_op jit(solution)/shard_map/chain/pallas_call | solution.py:504

commit v5 on v4

--- a/solution.py
+++ b/solution.py
@@ -16,9 +16,9 @@
 MESH = pl.DeviceIdType.MESH
 
 
-def patched(tile, halo_rows, f, j):
+def patched(tile, halo_rows, at, j):
     lane = lax.broadcasted_iota(jnp.int32, tile.shape, 1)
-    rolled = pltpu.roll(halo_rows, (128 - HALO_LANES[f] - j) % 128, 1)
+    rolled = pltpu.roll(halo_rows, (128 - at - j) % 128, 1)
     north = 111 if j < 4 else 110
     here = lane == 0 if j == 4 else (lane == 0) | (lane == north)
     return jnp.where(here, rolled, tile)
@@ -26,9 +26,9 @@
 
 def exchange_kernel(
     init_hbm, drag_hbm, dir_hbm, mask_hbm, cells_hbm, sign_hbm,
-    t_hbm, halo, from_west, from_east, w_hbm,
+    t_hbm, halo, corner, from_west, from_east, w_hbm,
     t_ref, w_ref, init_ref, drag_ref, dir_ref, mask_ref, cells_ref, sign_ref,
-    nat, edge, strip, north_tile, at_ref, acc, fold_acc, load_sem, send_sem, recv_sem, out_sem,
+    nat, north_tile, edge_tile, at_ref, acc, fold_acc, load_sem, send_sem, recv_sem, out_sem,
 ):
     rows, cols = drag_ref.shape
     ext = cols + 2 * PAD
@@ -49,7 +49,7 @@
 
     up_lat = jnp.where(top, lat, lat + 1)
     up_lon = jnp.where(top, n_lon - 1 - lon, lon)
-    up_slot = jnp.where(top, 3, 0)
+    up_half = jnp.where(top, 1, 0)
     turns = (0, 1, -1)
     ups = [around(up_lon, by) for by in turns]
     downs = [around(lon, by) for by in turns]
@@ -75,7 +75,12 @@
     for load in loads:
         load.start()
 
-    lane_of = lax.broadcasted_iota(jnp.int32, (64, cols), 1)
+    def beside(fields):
+        lane_of = lax.broadcasted_iota(jnp.int32, fields[0].shape, 1)
+        sides = pltpu.roll(fields[0], 8, 1)
+        for f in range(1, 5):
+            sides = jnp.where(lane_of < 16 * f, sides, pltpu.roll(fields[f], 16 * f + 8, 1))
+        return sides
 
     def prepare(part, carry):
         here = pl.ds(pl.multiple_of(part * 64, 64), 64)
@@ -89,14 +94,8 @@
             ocean * inverse,
             -(dir_ref[here, :] * inverse),
         ]
-        sides = pltpu.roll(fields[0], 8, 1)
         for f in range(5):
             nat[f, there, :] = fields[f]
-            if f:
-                sides = jnp.where(
-                    lane_of < 16 * f, sides, pltpu.roll(fields[f], 16 * f + 8, 1)
-                )
-        edge[there, :] = sides
         return carry
 
     height = nat.shape[1]
@@ -104,8 +103,6 @@
     for f in range(5):
         nat[f, 0:PAD, :] = jnp.zeros((PAD, cols), jnp.float32)
         nat[f, tail:, :] = jnp.zeros((height - tail, cols), jnp.float32)
-    edge[0:PAD, :] = jnp.zeros((PAD, cols), jnp.float32)
-    edge[tail:, :] = jnp.zeros((height - tail, cols), jnp.float32)
     for load in loads[:4]:
         load.wait()
     lax.fori_loop(0, rows // 64, prepare, 0)
@@ -125,19 +122,19 @@
             for k in range(PAD):
                 north_tile[f, k : k + 1, :] = turned[PAD - 1 - k : PAD - k, :]
 
-    def fill(src, slot):
-        return pltpu.make_async_copy(src, halo.at[slot], out_sem.at[2 + slot])
-
-    zeros = nat.at[:, pl.ds(tail, PAD), :]
+    edge_tile[0] = beside([north_tile[f] for f in range(5)])
+    edge_tile[1] = beside([nat[f, PAD : 2 * PAD, :] for f in range(5)])
+
+    def fill(src, dst, which):
+        return pltpu.make_async_copy(src, dst, out_sem.at[which])
+
     lowest = jnp.logical_not(inner)
-    for k in range(3):
-        pl.when(lowest)(fill(zeros, k).start)
-        pl.when(own_fold[k])(fill(north_tile, 3 + k).start)
-
-    for j in range(SLABS):
-        turned = edge[pl.ds(j + 1, 128, stride=SLABS), :].T
-        for f in range(5):
-            strip[j, f] = turned[16 * f : 16 * f + 16]
+    fills = [(lowest, fill(nat.at[:, pl.ds(tail, PAD), :], halo.at[0], 2))]
+    for k in range(2):
+        fills.append((lowest, fill(nat.at[0, pl.ds(tail, PAD), :], corner.at[k], 3 + k)))
+        fills.append((own_fold[1 + k], fill(edge_tile.at[0], corner.at[2 + k], 5 + k)))
+    for case, part in fills:
+        pl.when(case)(part.start)
 
     def copy(src, dst, which, slot, lon_at, lat_at):
         return pltpu.make_async_remote_copy(
@@ -146,33 +143,40 @@
             device_id_type=MESH,
         )
 
-    up_copies = [
-        copy(north_tile, halo.at[up_slot + k], k, up_slot + k, ups[k], up_lat)
-        for k in range(3)
+    up_copies = [copy(north_tile, halo.at[up_half], 0, up_half, ups[0], up_lat)]
+    down_copies = [
+        copy(nat.at[:, pl.ds(PAD, PAD), :], halo.at[1], 3, 1, downs[0], lat - 1)
     ]
-    down_copies = [
-        copy(nat.at[:, pl.ds(PAD, PAD), :], halo.at[3 + k], 3 + k, 3 + k, downs[k], lat - 1)
-        for k in range(3)
-    ]
+    for k in range(2):
+        slot = 2 * up_half + k
+        up_copies.append(
+            copy(edge_tile.at[0], corner.at[slot], 1 + k, 2 + slot, ups[1 + k], up_lat)
+        )
+        down_copies.append(
+            copy(
+                edge_tile.at[1], corner.at[2 + k], 4 + k, 4 + k,
+                downs[1 + k], lat - 1,
+            )
+        )
     east_copy = copy(
-        strip.at[:, pl.ds(0, 5), pl.ds(0, 8), :], from_west, 6, 6, around(lon, 1), lat
+        t_ref.at[:, :, pl.ds(cols - PAD, PAD), :], from_west, 6, 6, around(lon, 1), lat
     )
     west_copy = copy(
-        strip.at[:, pl.ds(0, 5), pl.ds(8, 8), :], from_east, 7, 7, around(lon, -1), lat
+        t_ref.at[:, :, pl.ds(0, PAD), :], from_east, 7, 7, around(lon, -1), lat
     )
-
-    pl.semaphore_wait(barrier, peers)
-    east_copy.start()
-    west_copy.start()
-    for k in (1, 2, 0):
-        pl.when(jnp.logical_not(own_fold[k]))(up_copies[k].start)
-        pl.when(inner)(down_copies[k].start)
 
     for f in range(5):
         for j in range(SLABS):
             t_ref[f, j] = nat[f, pl.ds(j + 1, 128, stride=SLABS), :].T
     own_out = pltpu.make_async_copy(t_ref, t_hbm, out_sem.at[0])
     own_out.start()
+
+    pl.semaphore_wait(barrier, peers)
+    for k in (1, 2, 0):
+        pl.when(jnp.logical_not(own_fold[k]))(up_copies[k].start)
+        pl.when(inner)(down_copies[k].start)
+    east_copy.start()
+    west_copy.start()
     for load in loads[4:]:
         load.wait()
 
@@ -214,24 +218,37 @@
             found.append(jnp.where(steps == at, hit, jnp.zeros((size, 128), jnp.bfloat16)))
         return jnp.concatenate(found, axis=1)
 
-    def gather_weights(part, carry):
-        first = part * CHUNK
-        signs = [
+    def signs_of(first):
+        return [
             jnp.broadcast_to(sign_ref[pl.ds(first + k, 1), :], (16, 128))
             .astype(jnp.float32).astype(jnp.bfloat16)
             for k in range(CHUNK)
         ]
+
+    def gather_weights(part, carry):
+        first = part * CHUNK
+        signs = signs_of(first)
         a = one_hot(0, first, 2 * ext)
         b = one_hot(1, first, LOW * 128, signs)
         acc[...] += lax.dot_general(a, b, contract, preferred_element_type=jnp.float32)
-        fa = one_hot(3, first, ext)
-        fb = one_hot(2, first, 16, signs)
-        fold_acc[:, 0:16] += lax.dot_general(
-            fa, fb, contract, preferred_element_type=jnp.float32
-        )
         return carry
 
     lax.fori_loop(0, cells_ref.shape[0] // CHUNK, gather_weights, 0)
+
+    @pl.when(top)
+    def _():
+        def gather_ghosts(part, carry):
+            first = part * CHUNK
+            signs = signs_of(first)
+            fa = one_hot(3, first, ext)
+            fb = one_hot(2, first, 16, signs)
+            fold_acc[:, 0:16] += lax.dot_general(
+                fa, fb, contract, preferred_element_type=jnp.float32
+            )
+            return carry
+
+        lax.fori_loop(0, cells_ref.shape[0] // CHUNK, gather_ghosts, 0)
+
     column = lax.broadcasted_iota(jnp.int32, (ext, 128), 1)
     ghosts = fold_acc[...]
     for j in range(SLABS):
@@ -246,15 +263,18 @@
     w_out = pltpu.make_async_copy(w_ref, w_hbm, out_sem.at[1])
     w_out.start()
 
+    pl.when(inner)(copy(north_tile, halo.at[0], 0, 0, ups[0], up_lat).wait_recv)
+    copy(north_tile, halo.at[1], 0, 1, ups[0], up_lat).wait_recv()
+    for k in range(2):
+        pl.when(inner)(
+            copy(edge_tile.at[0], corner.at[k], 1 + k, 2 + k, ups[1 + k], up_lat).wait_recv
+        )
+        pl.when(jnp.logical_not(own_fold[1 + k]))(
+            copy(edge_tile.at[0], corner.at[2 + k], 1 + k, 4 + k, ups[1 + k], up_lat).wait_recv
+        )
+    for case, part in fills:
+        pl.when(case)(part.wait)
     for k in range(3):
-        pl.when(inner)(
-            copy(north_tile, halo.at[k], k, k, ups[k], up_lat).wait_recv
-        )
-        pl.when(jnp.logical_not(own_fold[k]))(
-            copy(north_tile, halo.at[3 + k], k, 3 + k, ups[k], up_lat).wait_recv
-        )
-        pl.when(lowest)(fill(zeros, k).wait)
-        pl.when(own_fold[k])(fill(north_tile, 3 + k).wait)
         pl.when(jnp.logical_not(own_fold[k]))(up_copies[k].wait_send)
         pl.when(inner)(down_copies[k].wait_send)
     east_copy.wait_send()
@@ -266,8 +286,8 @@
 
 
 def chain_kernel(
-    t_hbm, halo_hbm, west_hbm, east_hbm, w_hbm, curv_hbm, state_hbm, tangent_hbm,
-    t_ref, halo, from_west, from_east, pack, patch, w_ref, levels, back_a, back_b, scale_ref, curv, nat, load_sem, out_sem,
+    t_hbm, halo_hbm, corner_hbm, west_hbm, east_hbm, w_hbm, curv_hbm, state_hbm, tangent_hbm,
+    t_ref, halo, corner, from_west, from_east, pack, patch, w_ref, levels, back_a, back_b, scale_ref, curv, nat, load_sem, out_sem,
 ):
     ext = t_ref.shape[2]
     cols = ext - 2 * PAD
@@ -277,17 +297,17 @@
     sides = [
         pltpu.make_async_copy(src, dst, load_sem.at[k])
         for k, (src, dst) in enumerate((
-            (halo_hbm, halo), (west_hbm, from_west), (east_hbm, from_east)
+            (halo_hbm, halo), (corner_hbm, corner), (west_hbm, from_west), (east_hbm, from_east)
         ))
     ]
     loads = [
         pltpu.make_async_copy(
             t_hbm.at[:, :, pl.ds(low, high - low), :],
-            t_ref.at[:, :, pl.ds(PAD + low, high - low), :], load_sem.at[3 + k],
+            t_ref.at[:, :, pl.ds(PAD + low, high - low), :], load_sem.at[4 + k],
         )
         for k, (low, high) in enumerate(zip(bounds, bounds[1:]))
     ]
-    w_load = pltpu.make_async_copy(w_hbm, w_ref, load_sem.at[6])
+    w_load = pltpu.make_async_copy(w_hbm, w_ref, load_sem.at[7])
     for load in sides + loads + [w_load]:
         load.start()
 
@@ -369,20 +389,28 @@
 
     pack[...] = jnp.zeros_like(pack)
     sides[0].wait()
-    for k in range(3):
+    sides[1].wait()
+
+    def place_rows(k, at, south, north):
+        pack[k, at : at + 7, :] = south[1:8]
+        pack[k, at - 17 : at - 13, :] = north[2:6]
+        pack[k, at - 13 : at - 11, :] = north[0:2]
+
+    for f in range(5):
+        place_rows(0, HALO_LANES[f], halo[0, f], halo[1, f])
+    for k in range(2):
+        place_rows(1 + k, HALO_LANES[0], corner[k], corner[2 + k])
+    patch[...] = pack[0].T
+    corners = pack[1].T, pack[2].T
+    sides[2].wait()
+    sides[3].wait()
+    for k, (got, place) in enumerate(((from_west, 0), (from_east, cols + PAD))):
         for f in range(5):
-            at = HALO_LANES[f]
-            pack[k, at : at + 7, :] = halo[k, f, 1:8, :]
-            pack[k, at - 17 : at - 13, :] = halo[3 + k, f, 2:6, :]
-            pack[k, at - 13 : at - 11, :] = halo[3 + k, f, 0:2, :]
-    patch[...] = pack[0].T
-    corners = pack[1].T[cols - PAD : cols], pack[2].T[0:PAD]
-    sides[1].wait()
-    sides[2].wait()
-    for got, corner, place in zip((from_west, from_east), corners, (0, cols + PAD)):
-        for f in range(5):
+            rows_in = corners[k][16 * f + 8 * k : 16 * f + 8 * k + 8]
             for j in range(SLABS):
-                t_ref[f, j, place : place + PAD, :] = patched(got[j, f], corner, f, j)
+                t_ref[f, j, place : place + PAD, :] = patched(
+                    got[f, j], rows_in, HALO_LANES[0], j
+                )
 
     for i in range(tiles):
         for load, low in zip(loads, bounds):
@@ -393,7 +421,9 @@
             halo_rows = patch[8 * i : 8 * i + 8, :]
             for f in range(5):
                 for j in range(SLABS):
-                    t_ref[f, j, here, :] = patched(t_ref[f, j, here, :], halo_rows, f, j)
+                    t_ref[f, j, here, :] = patched(
+                        t_ref[f, j, here, :], halo_rows, HALO_LANES[f], j
+                    )
         step(t_ref, levels.at[0], i, 0.25, first=True)
 
     def forward(n, carry):
@@ -464,14 +494,15 @@
     tall = SLABS * 128 + 8
     vm, dma = pltpu.VMEM, pltpu.SemaphoreType.DMA
     fields = jax.ShapeDtypeStruct((5, SLABS, cols, 128), f32)
-    halos = jax.ShapeDtypeStruct((6, 5, PAD, cols), f32)
-    beside = jax.ShapeDtypeStruct((SLABS, 5, PAD, 128), f32)
+    halos = jax.ShapeDtypeStruct((2, 5, PAD, cols), f32)
+    corners = jax.ShapeDtypeStruct((4, PAD, cols), f32)
+    beside = jax.ShapeDtypeStruct((5, SLABS, PAD, 128), f32)
     weights = jax.ShapeDtypeStruct((SLABS, ext, 128), f32)
     given = pl.pallas_call(
         exchange_kernel,
-        out_shape=(fields, halos, beside, beside, weights),
+        out_shape=(fields, halos, corners, beside, beside, weights),
         in_specs=[hbm] * 6,
-        out_specs=(hbm,) * 5,
+        out_specs=(hbm,) * 6,
         scratch_shapes=[
             vm(fields.shape, f32),
             vm(weights.shape, f32),
@@ -482,9 +513,8 @@
             vm((lines, 128), i32),
             vm((lines, 128), i32),
             vm((5, tall, cols), f32),
-            vm((tall, cols), f32),
-            vm((SLABS, 5, 16, 128), f32),
             vm((5, PAD, cols), f32),
+            vm((2, PAD, cols), f32),
             vm((4, lines, 128), i32),
             vm((2 * ext, LOW * 128), f32),
             vm((ext, 128), f32),
@@ -508,11 +538,12 @@
             jax.ShapeDtypeStruct((3, rows, cols), f32),
             jax.ShapeDtypeStruct((3, rows, cols), f32),
         ),
-        in_specs=[hbm] * 5,
+        in_specs=[hbm] * 6,
         out_specs=(hbm, hbm, hbm),
         scratch_shapes=[
             vm((5, SLABS, ext, 128), f32),
             vm(halos.shape, f32),
+            vm(corners.shape, f32),
             vm(beside.shape, f32),
             vm(beside.shape, f32),
             vm((3, 128, cols), f32),
@@ -524,7 +555,7 @@
             vm((SLABS, ext, 128), f32),
             vm((SLABS, cols, 128), f32),
             vm((7, tall, cols), f32),
-            dma((7,)),
+            dma((8,)),
             dma((7,)),
         ],
         compiler_params=pltpu.CompilerParams(vmem_limit_bytes=56 * 1024 * 1024),

time: 30.4 us -> 27.5 us (0.905)
  Pallas kernels: 29.6 us -> 26.7 us
    pallas_call x1, Pallas kernels: 18.3 us -> 15.4 us  [on_device(): pl.pallas_call(exchange_kernel, out_shape=(fields, halos, corners, beside...]
where the time goes in v5:
time: 27.5 us; the launch traced here: 27.3 us
  Pallas kernels  26.7 us (97%)
  between operations  0.64 us (2%)
    pallas_call x1, Pallas kernels, on_device(): pl.pallas_call(exchange_kernel, out_shape=(fields, halos, corners, beside...  15.4 us
    pallas_call x1, Pallas kernels, on_device(): pl.pallas_call(chain_kernel, out_shape=(jax.ShapeDtypeStruct((rows, cols)...  11.3 us

profile of v5, /device:TPU:1, one launch (start us, length us, event | category | flops | bytes accessed | tf_op | source)
XLA Modules:
  0.0 27.3 jit_solution(9666498949625361522)
XLA Ops:
  0.6 15.4 %exchange.1 = (f32[5,7,128,128]{3,2,1,0:T(8,128)}, f32[2,5,8,128]{3,2,1,0:T(8,128)}, f32[4,8,128]{2,1,0:T(8,128)}, f32[5,7,8,128]{3,2,1,0:T(8,128)}, f32[5,7,8,128]{3,2,1,0:T(8,128)}, /*index=5*/f32[7,144,128]{2,1,0:T(8,128)}) custom-call(f32[3,768,128]{2,1,0:T(8,128)} %init_hbm.1, f32[768,128]{1,0:T(8,128)} %drag_hbm.1, f32[768,128]{1,0:T(8,128)} %dir_hbm.1, ...), custom_call_target="tpu_custom_call" | custom-call | tf_op jit(solution)/shard_map/exchange/pallas_call | solution.py:501
  16.1 11.3 %chain.1 = (f32[768,128]{1,0:T(8,128)}, f32[3,768,128]{2,1,0:T(8,128)}, f32[3,768,128]{2,1,0:T(8,128)}) custom-call(f32[5,7,128,128]{3,2,1,0:T(8,128)} %get-tuple-element.9.t_hbm, f32[2,5,8,128]{3,2,1,0:T(8,128)} %get-tuple-element.10.halo_hbm, f32[4,8,128]{2,1,0:T(8,128)} %get-tuple-element.11.corner_hbm, f32[5,7,8,128]{3,2,1,0:T(8,128)} %get-tuple-element.12.west_hbm, ...), custom_call_target="tpu_custom_call" | custom-call | tf_op jit(solution)/shard_map/chain/pallas_call | solution.py:534

commit v6 on v5

--- a/solution.py
+++ b/solution.py
@@ -159,10 +159,11 @@
             )
         )
     east_copy = copy(
-        t_ref.at[:, :, pl.ds(cols - PAD, PAD), :], from_west, 6, 6, around(lon, 1), lat
+        t_ref.at[:, :, pl.ds(cols - ITERS, ITERS), :],
+        from_west.at[:, :, pl.ds(PAD - ITERS, ITERS), :], 6, 6, around(lon, 1), lat
     )
     west_copy = copy(
-        t_ref.at[:, :, pl.ds(0, PAD), :], from_east, 7, 7, around(lon, -1), lat
+        t_ref.at[:, :, pl.ds(0, ITERS), :], from_east.at[:, :, pl.ds(0, ITERS), :], 7, 7, around(lon, -1), lat
     )
 
     for f in range(5):
@@ -216,7 +217,7 @@
             else:
                 hit = jnp.concatenate([value[k]] * (size // 16), axis=0)
             found.append(jnp.where(steps == at, hit, jnp.zeros((size, 128), jnp.bfloat16)))
-        return jnp.concatenate(found, axis=1)
+        return jnp.concatenate(found, axis=1).astype(jnp.float8_e4m3fn)
 
     def signs_of(first):
         return [
@@ -404,12 +405,15 @@
     corners = pack[1].T, pack[2].T
     sides[2].wait()
     sides[3].wait()
+    line = lax.broadcasted_iota(jnp.int32, (PAD, 128), 0)
+    sent = line >= PAD - ITERS, line < ITERS
     for k, (got, place) in enumerate(((from_west, 0), (from_east, cols + PAD))):
         for f in range(5):
             rows_in = corners[k][16 * f + 8 * k : 16 * f + 8 * k + 8]
             for j in range(SLABS):
+                tile = jnp.where(sent[k], got[f, j], 0.0)
                 t_ref[f, j, place : place + PAD, :] = patched(
-                    got[f, j], rows_in, HALO_LANES[0], j
+                    tile, rows_in, HALO_LANES[0], j
                 )
 
     for i in range(tiles):

time: 27.5 us -> 26.7 us (0.971)
  Pallas kernels: 26.7 us -> 25.9 us
    pallas_call x1, Pallas kernels: 15.4 us -> 14.6 us  [on_device(): pl.pallas_call(exchange_kernel, out_shape=(fields, halos, corners, beside...]
where the time goes in v6:
time: 26.7 us; the launch traced here: 26.5 us
  Pallas kernels  25.9 us (97%)
  between operations  0.64 us (2%)
    pallas_call x1, Pallas kernels, on_device(): pl.pallas_call(exchange_kernel, out_shape=(fields, halos, corners, beside...  14.6 us
    pallas_call x1, Pallas kernels, on_device(): pl.pallas_call(chain_kernel, out_shape=(jax.ShapeDtypeStruct((rows, cols)...  11.3 us

profile of v6, /device:TPU:1, one launch (start us, length us, event | category | flops | bytes accessed | tf_op | source)
XLA Modules:
  0.0 26.5 jit_solution(5060770925500388910)
XLA Ops:
  0.6 14.6 %exchange.1 = (f32[5,7,128,128]{3,2,1,0:T(8,128)}, f32[2,5,8,128]{3,2,1,0:T(8,128)}, f32[4,8,128]{2,1,0:T(8,128)}, f32[5,7,8,128]{3,2,1,0:T(8,128)}, f32[5,7,8,128]{3,2,1,0:T(8,128)}, /*index=5*/f32[7,144,128]{2,1,0:T(8,128)}) custom-call(f32[3,768,128]{2,1,0:T(8,128)} %init_hbm.1, f32[768,128]{1,0:T(8,128)} %drag_hbm.1, f32[768,128]{1,0:T(8,128)} %dir_hbm.1, ...), custom_call_target="tpu_custom_call" | custom-call | tf_op jit(solution)/shard_map/exchange/pallas_call | solution.py:505
  15.3 11.3 %chain.1 = (f32[768,128]{1,0:T(8,128)}, f32[3,768,128]{2,1,0:T(8,128)}, f32[3,768,128]{2,1,0:T(8,128)}) custom-call(f32[5,7,128,128]{3,2,1,0:T(8,128)} %get-tuple-element.9.t_hbm, f32[2,5,8,128]{3,2,1,0:T(8,128)} %get-tuple-element.10.halo_hbm, f32[4,8,128]{2,1,0:T(8,128)} %get-tuple-element.11.corner_hbm, f32[5,7,8,128]{3,2,1,0:T(8,128)} %get-tuple-element.12.west_hbm, ...), custom_call_target="tpu_custom_call" | custom-call | tf_op jit(solution)/shard_map/chain/pallas_call | solution.py:538

commit v7 on v6

--- a/solution.py
+++ b/solution.py
@@ -252,6 +252,7 @@
 
     column = lax.broadcasted_iota(jnp.int32, (ext, 128), 1)
     ghosts = fold_acc[...]
+    w_outs = []
     for j in range(SLABS):
         hi, lo = divmod(j, LOW)
         found = acc[hi * ext : (hi + 1) * ext, lo * 128 : (lo + 1) * 128]
@@ -261,8 +262,8 @@
                 turned = pltpu.roll(ghosts, lane_at - k, 1)
                 found -= jnp.where(column == lane_at, turned, 0.0)
         w_ref[j] = found
-    w_out = pltpu.make_async_copy(w_ref, w_hbm, out_sem.at[1])
-    w_out.start()
+        w_outs.append(pltpu.make_async_copy(w_ref.at[j], w_hbm.at[j], out_sem.at[7 + j]))
+        w_outs[j].start()
 
     pl.when(inner)(copy(north_tile, halo.at[0], 0, 0, ups[0], up_lat).wait_recv)
     copy(north_tile, halo.at[1], 0, 1, ups[0], up_lat).wait_recv()
@@ -281,7 +282,8 @@
     east_copy.wait_send()
     west_copy.wait_send()
     own_out.wait()
-    w_out.wait()
+    for w_out in w_outs:
+        w_out.wait()
     east_copy.wait_recv()
     west_copy.wait_recv()
 
@@ -525,7 +527,7 @@
             dma((6,)),
             dma((8,)),
             dma((8,)),
-            dma((8,)),
+            dma((7 + SLABS,)),
         ],
         compiler_params=pltpu.CompilerParams(
             collective_id=0, has_side_effects=True, vmem_limit_bytes=56 * 1024 * 1024

time: 26.7 us -> 26.8 us (level)
  no operation moved by 1% of the time
where the time goes in v7:
time: 26.8 us; the launch traced here: 26.6 us
  Pallas kernels  26 us (97%)
  between operations  0.64 us (2%)
    pallas_call x1, Pallas kernels, on_device(): pl.pallas_call(exchange_kernel, out_shape=(fields, halos, corners, beside...  14.7 us
    pallas_call x1, Pallas kernels, on_device(): pl.pallas_call(chain_kernel, out_shape=(jax.ShapeDtypeStruct((rows, cols)...  11.3 us

profile of v7, /device:TPU:1, one launch (start us, length us, event | category | flops | bytes accessed | tf_op | source)
XLA Modules:
  0.0 26.6 jit_solution(17469786603274211490)
XLA Ops:
  0.6 14.7 %exchange.1 = (f32[5,7,128,128]{3,2,1,0:T(8,128)}, f32[2,5,8,128]{3,2,1,0:T(8,128)}, f32[4,8,128]{2,1,0:T(8,128)}, f32[5,7,8,128]{3,2,1,0:T(8,128)}, f32[5,7,8,128]{3,2,1,0:T(8,128)}, /*index=5*/f32[7,144,128]{2,1,0:T(8,128)}) custom-call(f32[3,768,128]{2,1,0:T(8,128)} %init_hbm.1, f32[768,128]{1,0:T(8,128)} %drag_hbm.1, f32[768,128]{1,0:T(8,128)} %dir_hbm.1, ...), custom_call_target="tpu_custom_call" | custom-call | tf_op jit(solution)/shard_map/exchange/pallas_call | solution.py:507
  15.3 11.3 %chain.1 = (f32[768,128]{1,0:T(8,128)}, f32[3,768,128]{2,1,0:T(8,128)}, f32[3,768,128]{2,1,0:T(8,128)}) custom-call(f32[5,7,128,128]{3,2,1,0:T(8,128)} %get-tuple-element.9.t_hbm, f32[2,5,8,128]{3,2,1,0:T(8,128)} %get-tuple-element.10.halo_hbm, f32[4,8,128]{2,1,0:T(8,128)} %get-tuple-element.11.corner_hbm, f32[5,7,8,128]{3,2,1,0:T(8,128)} %get-tuple-element.12.west_hbm, ...), custom_call_target="tpu_custom_call" | custom-call | tf_op jit(solution)/shard_map/chain/pallas_call | solution.py:540
